TPU v7x, 256 devices: a whole 4x4x8 slice. The times are simulated.
256 devices in a mesh: gx: 8 (over x, core), gy: 16 (over z_hi, y), gz: 2 (over z_lo).
Axes of the slice: x: 4, y: 4, z: 8 (z_hi: 4, z_lo: 2; z = z_hi * 2 + z_lo), core: 2. Of those that a mesh axis runs over, the one named last changes fastest.
Arguments:
- kelvin_before_scan: float32 [128, 512, 256], P('gx', 'gy', 'gz'), may hold values from -5 to 5
- conductance_coefficient: float32 [128, 512, 256], P('gx', 'gy', 'gz'), may hold values from 0.8 to 1
- remelted_flag: int32 [128, 512, 256], P('gx', 'gy', 'gz'), may hold values 0 or 1
- germ_site_flag: int32 [128, 512, 256], P('gx', ('gy', 'gz')), may hold values 0 or 1
- nucleus_grain_label: int32 [128, 512, 256], P('gx', ('gy', 'gz')), may hold values from 1 to 8192
- lattice_pose_number: int32 [128, 512, 256], P('gx', ('gy', 'gz')), may hold values from 0 to 63
- engulf_outcome: int32 [2, 128, 512, 256], P(None, 'gx', ('gy', 'gz')), may hold values from 0 to 6, as said below
- expanding_patch_roster: int32 [8, 32, 8], P('gx', ('gy', 'gz')), may hold values from -1 to 7, as said below
- lattice_pose_turns: float32 [3, 64], replicated, may hold values from -3.140625 to 3.140625
Outputs:
- temperature_out: float32 [128, 512, 256], P('gx', 'gy', 'gz')
- envelope: float32 [128, 512, 256], P('gx', ('gy', 'gz'))
- grain_map: int32 [128, 512, 256], P('gx', ('gy', 'gz'))
Inputs may be any that keep to these rules, and one draw needn't show every extreme that they name: `engulf_outcome`: 0 means no capture in that step; 1 to 6 name the capturing neighbour: -x, +x, -y, +y, -z, +z in that order. `expanding_patch_roster`: each device's row starts with 1 to 8 distinct tile numbers of 0 to 7 and is filled up with -1; some device lists all 8 tiles.
All inputs are finite; a program needn't handle non-finite values. No bound on the sum of `remelted_flag` or of `germ_site_flag` on one device may be relied on, other than what follows from the above.
Results may differ from a plain program's by a relative error of at most 0.0004.
Values sent between devices are 32-bit elements; how exact they have to be, the bound alone decides.
A program may use at most 64 MiB of HBM per device.

v0:
```python
import jax
import jax.numpy as jnp
from jax import lax
from jax.sharding import PartitionSpec as P

SUBSTEPS = 6


FREEZE_RELEASE = 2.0
LIQUID_BOOST = 0.5
TIME_STEP = 0.1
SCAN_LINE_INPUT = 1.5
POWDER_SHARE = 0.25
GROWTH_COEF = 1.0


def extended(cells, sides, width):
    for axis, dim in sides:
        count = lax.axis_size(axis)
        ends = count - 1
        head = lax.slice_in_dim(cells, 0, width, axis=dim)
        tail = lax.slice_in_dim(cells, cells.shape[dim] - width, cells.shape[dim], axis=dim)
        cells = jnp.concatenate(
            [
                lax.ppermute(tail, axis, [(i, (i + 1) % count) for i in range(ends)]),
                cells,
                lax.ppermute(head, axis, [((i + 1) % count, i) for i in range(ends)]),
            ],
            axis=dim,
        )
    return cells


def melting_point(stored_caloric_content):
    return jnp.where(
        stored_caloric_content < 0.0,
        stored_caloric_content,
        jnp.where(
            stored_caloric_content > 1.0 + FREEZE_RELEASE,
            stored_caloric_content - FREEZE_RELEASE,
            stored_caloric_content / (1.0 + FREEZE_RELEASE),
        ),
    )


def face_flux(center_t, center_k, other_t, other_k):
    denominator = center_k + other_k
    safe_denom = jnp.where(denominator > 0.0, denominator, 1.0)
    return 2.0 * center_k * other_k / safe_denom * (other_t - center_t)


def heat_substep(padded_heat, cond_pad):
    current_fields = melting_point(padded_heat)
    conducts = cond_pad * (1.0 + LIQUID_BOOST * jnp.clip(current_fields, 0.0, 1.0))
    center_t = current_fields[1:-1, 1:-1, 1:-1]
    center_k = conducts[1:-1, 1:-1, 1:-1]
    shifts = (
        (slice(None, -2), slice(1, -1), slice(1, -1)),
        (slice(2, None), slice(1, -1), slice(1, -1)),
        (slice(1, -1), slice(None, -2), slice(1, -1)),
        (slice(1, -1), slice(2, None), slice(1, -1)),
        (slice(1, -1), slice(1, -1), slice(None, -2)),
        (slice(1, -1), slice(1, -1), slice(2, None)),
    )
    flux_total = jnp.zeros_like(center_t)
    for window in shifts:
        flux_total = flux_total + face_flux(
            center_t, center_k, current_fields[window], conducts[window]
        )
    return padded_heat[1:-1, 1:-1, 1:-1] + TIME_STEP * flux_total


def envelope_reach(angles):
    cos_a, sin_a = (jnp.cos(angles[0]), jnp.sin(angles[0]))
    cos_b, sin_b = (jnp.cos(angles[1]), jnp.sin(angles[1]))
    cos_c, sin_c = (jnp.cos(angles[2]), jnp.sin(angles[2]))
    row_x = (
        jnp.abs(cos_a * cos_c - sin_a * sin_c * cos_b)
        + jnp.abs(-cos_a * sin_c - sin_a * cos_c * cos_b)
        + jnp.abs(sin_a * sin_b)
    )
    row_y = (
        jnp.abs(sin_a * cos_c + cos_a * sin_c * cos_b)
        + jnp.abs(-sin_a * sin_c + cos_a * cos_c * cos_b)
        + jnp.abs(-cos_a * sin_b)
    )
    row_z = jnp.abs(sin_c * sin_b) + jnp.abs(cos_c * sin_b) + jnp.abs(cos_b)
    return jnp.stack([row_x, row_y, row_z])


def growth_speed(cooling, liquid_time):
    undercool = jnp.maximum(cooling, 0.0) * (0.5 + liquid_time)
    return GROWTH_COEF * undercool * undercool


def pick_side(tile_block, capture_code):
    center = tile_block[1:-1, 1:-1, :]
    zero_face = jnp.zeros_like(center[:, :, :1])
    views = (
        tile_block[:-2, 1:-1, :],
        tile_block[2:, 1:-1, :],
        tile_block[1:-1, :-2, :],
        tile_block[1:-1, 2:, :],
        jnp.concatenate([zero_face, center[:, :, :-1]], axis=2),
        jnp.concatenate([center[:, :, 1:], zero_face], axis=2),
    )
    picked = jnp.zeros_like(center)
    for number, window_view in enumerate(views):
        picked = jnp.where(capture_code == number + 1, window_view, picked)
    return picked


def reach_lookup(reach, orients, axis_code, pieces):
    flat_o = orients.reshape(pieces, -1)
    flat_a = axis_code.reshape(pieces, -1)
    table_ids = jnp.arange(reach.shape[1], dtype=jnp.int32)

    def one_piece(piece_pair):
        orient_row, axis_row = piece_pair
        onehot = (table_ids[:, None] == orient_row[None, :]).astype(jnp.float32)
        distances = jnp.dot(
            reach, onehot, precision=lax.Precision.HIGHEST, preferred_element_type=jnp.float32
        )
        return jnp.where(
            axis_row == 0, distances[0], jnp.where(axis_row == 1, distances[1], distances[2])
        )

    return lax.map(one_piece, (flat_o, flat_a)).reshape(orients.shape)


def advance(tile_block, capture_code, old_label, reach, pieces):
    grown_block = tile_block[0]
    label_block = tile_block[1]
    grown_center = grown_block[1:-1, 1:-1, :]
    side_grown = pick_side(grown_block, capture_code)
    side_label = pick_side(label_block, capture_code).astype(jnp.int32)
    table_size = reach.shape[1]
    side_reach = reach_lookup(reach, side_label % table_size, (capture_code - 1) // 2, pieces)
    captured = jnp.maximum(side_grown - side_reach, 0.0)
    taken = capture_code > 0
    return (jnp.where(taken, captured, grown_center), jnp.where(taken, side_label, old_label))


def sweep_listed(wide, capture_code, envelope, label, listed, rows_tile, reach):
    live_count = jnp.sum((listed >= 0).astype(jnp.int32))

    def visit_tile(visit_index, loop_state):
        env_now, label_now = loop_state
        start_row = listed[visit_index] * rows_tile
        tile_block = lax.dynamic_slice_in_dim(wide, start_row, rows_tile + 2, 1)
        code_rows = lax.dynamic_slice_in_dim(capture_code, start_row, rows_tile, 0)
        label_rows = lax.dynamic_slice_in_dim(label, start_row, rows_tile, 0)
        new_env, new_label = advance(tile_block, code_rows, label_rows, reach, 1)
        return (
            lax.dynamic_update_slice_in_dim(env_now, new_env, start_row, 0),
            lax.dynamic_update_slice_in_dim(label_now, new_label, start_row, 0),
        )

    return lax.fori_loop(0, live_count, visit_tile, (envelope, label))


def body(
    kelvin_before_scan,
    conductance_coefficient,
    remelted_flag,
    germ_site_flag,
    nucleus_grain_label,
    lattice_pose_number,
    engulf_outcome,
    expanding_patch_roster,
    lattice_pose_turns,
):
    molten_proportion = remelted_flag.astype(jnp.float32)
    base_cond = conductance_coefficient * (POWDER_SHARE + (1.0 - POWDER_SHARE) * molten_proportion)
    opening_kelvin_level = kelvin_before_scan + SCAN_LINE_INPUT * molten_proportion
    stored_caloric_content = opening_kelvin_level + FREEZE_RELEASE * jnp.clip(
        opening_kelvin_level, 0.0, 1.0
    )
    thermal_history = []
    cond_pad = extended(base_cond, (("gx", 0), ("gy", 1), ("gz", 2)), 1)
    for step_index in range(SUBSTEPS):
        padded_heat = extended(stored_caloric_content, (("gx", 0), ("gy", 1), ("gz", 2)), 1)
        stored_caloric_content = heat_substep(padded_heat, cond_pad)
        thermal_history.append(melting_point(stored_caloric_content))
    liquid_sum = jnp.zeros_like(thermal_history[0])
    for current_fields in thermal_history:
        liquid_sum = liquid_sum + jnp.clip(current_fields, 0.0, 1.0)
    liquid_time = TIME_STEP * liquid_sum
    cooling = (thermal_history[-2] - thermal_history[-1]) / TIME_STEP
    tile_cooling, tile_liquid = (
        lax.all_to_all(cooling, "gz", split_axis=1, concat_axis=2, tiled=True),
        lax.all_to_all(liquid_time, "gz", split_axis=1, concat_axis=2, tiled=True),
    )
    speed = growth_speed(tile_cooling, tile_liquid)
    reach = envelope_reach(lattice_pose_turns)
    table_size = lattice_pose_turns.shape[1]
    label = germ_site_flag * (nucleus_grain_label * table_size + lattice_pose_number)
    envelope = jnp.zeros(speed.shape, jnp.float32)
    listed = expanding_patch_roster.reshape(-1)
    rows_tile = envelope.shape[0] // expanding_patch_roster.shape[2]
    for growth_index in range(2):
        capture_code = engulf_outcome[growth_index]
        grown = envelope + jnp.where(label > 0, speed, 0.0)
        stacked = jnp.stack([grown, label.astype(jnp.float32)])
        wide = extended(stacked, (("gx", 1), (("gy", "gz"), 2)), 1)
        envelope, label = sweep_listed(
            wide, capture_code, envelope, label, listed, rows_tile, reach
        )
    return (thermal_history[-1], envelope, label // table_size)


def solution(mesh):
    placed = (
        P("gx", "gy", "gz"),
        P("gx", "gy", "gz"),
        P("gx", "gy", "gz"),
        P("gx", ("gy", "gz"), None),
        P("gx", ("gy", "gz"), None),
        P("gx", ("gy", "gz"), None),
        P(None, "gx", ("gy", "gz"), None),
        P("gx", ("gy", "gz"), None),
        P(),
    )
    return jax.shard_map(
        body,
        mesh=mesh,
        in_specs=placed,
        out_specs=(P("gx", "gy", "gz"), P("gx", ("gy", "gz"), None), P("gx", ("gy", "gz"), None)),
        check_vma=False,
    )
```

profile of v0, /device:TPU:128, one launch (start us, length us, event | category | flops | bytes accessed | tf_op | source)
XLA Modules:
  0.0 340.8 jit_solution(12308989096780812242)
XLA Ops:
  0.6 1.6 copy_multiply_fusion
  2.3 1.7 collective-permute-start
  5.4 4.3 %collective-permute-start.6 = (f32[1,32,128]{2,0,1:T(1,128)S(1)}, f32[1,32,128]{2,0,1:T(1,128)S(1)}, u32[]{:S(2)}, u32[]{:S(2)}) collective-permute-start(f32[1,32,128]{2,0,1:T(1,128)S(1)} %get-tuple-element.488), channel_id=1, source_target_pairs={{0,32},{32,64},{64,96},{96,128},{128,160},{160,192},{192,224},{1,3... | collective-permute-start | bytes 49160 | tf_op jit(solution)/shard_map/ppermute | solution.py:25
  11.0 3.5 %collective-permute-start.2 = (f32[18,1,128]{2,0,1:T(8,128)S(1)}, f32[18,1,128]{2,0,1:T(8,128)S(1)}, u32[]{:S(2)}, u32[]{:S(2)}) collective-permute-start(f32[18,1,128]{2,0,1:T(8,128)S(1)} %get-tuple-element.476), channel_id=1, source_target_pairs={{0,2},{2,4},{4,6},{6,8},{8,10},{10,12},{12,14},{14,16},{16,18},{18... | collective-permute-start | bytes 27656 | tf_op jit(solution)/shard_map/ppermute | solution.py:25
  14.5 6.6 %collective-permute-start.3 = (f32[18,1,128]{2,0,1:T(8,128)S(1)}, f32[18,1,128]{2,0,1:T(8,128)S(1)}, u32[]{:S(2)}, u32[]{:S(2)}) collective-permute-start(f32[18,1,128]{2,0,1:T(8,128)S(1)} %get-tuple-element.477), channel_id=1, source_target_pairs={{2,0},{4,2},{6,4},{8,6},{10,8},{12,10},{14,12},{16,14},{18,16},{20... | collective-permute-start | bytes 27656 | tf_op jit(solution)/shard_map/ppermute | solution.py:27
  21.1 1.9 collective-permute-start.8
  23.1 8.1 %collective-permute-start.9 = (f32[18,1,128]{2,0,1:T(8,128)S(1)}, f32[18,1,128]{2,0,1:T(8,128)S(1)}, u32[]{:S(2)}, u32[]{:S(2)}) collective-permute-start(f32[18,1,128]{2,0,1:T(8,128)S(1)} %get-tuple-element.475), channel_id=1, source_target_pairs={{2,0},{4,2},{6,4},{8,6},{10,8},{12,10},{14,12},{16,14},{18,16},{20... | collective-permute-start | bytes 27656 | tf_op jit(solution)/shard_map/ppermute | solution.py:27
  31.5 2.9 collective-permute-start.4
  36.0 4.6 %collective-permute-start.10 = (f32[18,34,1]{2,0,1:T(8,128)S(1)}, f32[18,34,1]{2,0,1:T(8,128)S(1)}, u32[]{:S(2)}, u32[]{:S(2)}) collective-permute-start(f32[18,34,1]{2,0,1:T(8,128)S(1)} %get-tuple-element.460), channel_id=1, source_target_pairs={{0,1},{2,3},{4,5},{6,7},{8,9},{10,11},{12,13},{14,15},{16,17},{18,... | collective-permute-start | bytes 7352 | tf_op jit(solution)/shard_map/ppermute | solution.py:25
  41.9 2.2 collective-permute-done.4
  44.2 4.7 %collective-permute-done.5 = f32[18,34,1]{2,0,1:T(8,128)S(1)} collective-permute-done((f32[18,34,1]{2,0,1:T(8,128)S(1)}, f32[18,34,1]{2,0,1:T(8,128)S(1)}, u32[]{:S(2)}, u32[]{:S(2)}) %collective-permute-start.5) | collective-permute-done | bytes 2480 | tf_op jit(solution)/shard_map/ppermute | solution.py:27
  48.9 4.3 %collective-permute-done.10 = f32[18,34,1]{2,0,1:T(8,128)S(1)} collective-permute-done((f32[18,34,1]{2,0,1:T(8,128)S(1)}, f32[18,34,1]{2,0,1:T(8,128)S(1)}, u32[]{:S(2)}, u32[]{:S(2)}) %collective-permute-start.10) | collective-permute-done | bytes 2480 | tf_op jit(solution)/shard_map/ppermute | solution.py:25
  53.1 4.7 %collective-permute-done.11 = f32[18,34,1]{2,0,1:T(8,128)S(1)} collective-permute-done((f32[18,34,1]{2,0,1:T(8,128)S(1)}, f32[18,34,1]{2,0,1:T(8,128)S(1)}, u32[]{:S(2)}, u32[]{:S(2)}) %collective-permute-start.11) | collective-permute-done | bytes 2480 | tf_op jit(solution)/shard_map/ppermute | solution.py:27
  59.8 2.0 collective-permute-start.12
  63.1 2.8 collective-permute-done.13
  65.9 1.9 collective-permute-start.14
  67.8 8.1 %collective-permute-start.15 = (f32[18,1,128]{2,0,1:T(8,128)S(1)}, f32[18,1,128]{2,0,1:T(8,128)S(1)}, u32[]{:S(2)}, u32[]{:S(2)}) collective-permute-start(f32[18,1,128]{2,0,1:T(8,128)S(1)} %get-tuple-element.473), channel_id=1, source_target_pairs={{2,0},{4,2},{6,4},{8,6},{10,8},{12,10},{14,12},{16,14},{18,16},{20... | collective-permute-start | bytes 27656 | tf_op jit(solution)/shard_map/ppermute | solution.py:27
  76.0 1.4 collective-permute-done.15
  77.6 1.5 collective-permute-start.16
  80.4 8.3 %collective-permute-done.16 = f32[18,34,1]{2,0,1:T(8,128)S(1)} collective-permute-done((f32[18,34,1]{2,0,1:T(8,128)S(1)}, f32[18,34,1]{2,0,1:T(8,128)S(1)}, u32[]{:S(2)}, u32[]{:S(2)}) %collective-permute-start.16) | collective-permute-done | bytes 2480 | tf_op jit(solution)/shard_map/ppermute | solution.py:25
  88.6 4.6 %collective-permute-done.17 = f32[18,34,1]{2,0,1:T(8,128)S(1)} collective-permute-done((f32[18,34,1]{2,0,1:T(8,128)S(1)}, f32[18,34,1]{2,0,1:T(8,128)S(1)}, u32[]{:S(2)}, u32[]{:S(2)}) %collective-permute-start.17) | collective-permute-done | bytes 2480 | tf_op jit(solution)/shard_map/ppermute | solution.py:27
  95.2 2.0 collective-permute-start.18
  98.5 2.9 collective-permute-done.19
  101.5 1.9 collective-permute-start.20
  103.4 8.4 %collective-permute-start.21 = (f32[18,1,128]{2,0,1:T(8,128)S(1)}, f32[18,1,128]{2,0,1:T(8,128)S(1)}, u32[]{:S(2)}, u32[]{:S(2)}) collective-permute-start(f32[18,1,128]{2,0,1:T(8,128)S(1)} %get-tuple-element.471), channel_id=1, source_target_pairs={{2,0},{4,2},{6,4},{8,6},{10,8},{12,10},{14,12},{16,14},{18,16},{20... | collective-permute-start | bytes 27656 | tf_op jit(solution)/shard_map/ppermute | solution.py:27
  111.8 1.4 collective-permute-done.21
  113.5 1.5 collective-permute-start.22
  116.3 7.9 %collective-permute-done.22 = f32[18,34,1]{2,0,1:T(8,128)S(1)} collective-permute-done((f32[18,34,1]{2,0,1:T(8,128)S(1)}, f32[18,34,1]{2,0,1:T(8,128)S(1)}, u32[]{:S(2)}, u32[]{:S(2)}) %collective-permute-start.22) | collective-permute-done | bytes 2480 | tf_op jit(solution)/shard_map/ppermute | solution.py:25
  124.2 4.7 %collective-permute-done.23 = f32[18,34,1]{2,0,1:T(8,128)S(1)} collective-permute-done((f32[18,34,1]{2,0,1:T(8,128)S(1)}, f32[18,34,1]{2,0,1:T(8,128)S(1)}, u32[]{:S(2)}, u32[]{:S(2)}) %collective-permute-start.23) | collective-permute-done | bytes 2480 | tf_op jit(solution)/shard_map/ppermute | solution.py:27
  130.9 2.2 collective-permute-start.24
  134.4 2.2 collective-permute-done.25
  136.6 1.9 collective-permute-start.26
  138.5 8.2 %collective-permute-start.27 = (f32[18,1,128]{2,0,1:T(8,128)S(1)}, f32[18,1,128]{2,0,1:T(8,128)S(1)}, u32[]{:S(2)}, u32[]{:S(2)}) collective-permute-start(f32[18,1,128]{2,0,1:T(8,128)S(1)} %get-tuple-element.469), channel_id=1, source_target_pairs={{2,0},{4,2},{6,4},{8,6},{10,8},{12,10},{14,12},{16,14},{18,16},{20... | collective-permute-start | bytes 27656 | tf_op jit(solution)/shard_map/ppermute | solution.py:27
  146.8 1.4 collective-permute-done.27
  148.4 1.5 collective-permute-start.28
  149.9 1.5 collective-permute-start.29
  151.4 7.8 %collective-permute-done.28 = f32[18,34,1]{2,0,1:T(8,128)S(1)} collective-permute-done((f32[18,34,1]{2,0,1:T(8,128)S(1)}, f32[18,34,1]{2,0,1:T(8,128)S(1)}, u32[]{:S(2)}, u32[]{:S(2)}) %collective-permute-start.28) | collective-permute-done | bytes 2480 | tf_op jit(solution)/shard_map/ppermute | solution.py:25
  159.2 4.7 %collective-permute-done.29 = f32[18,34,1]{2,0,1:T(8,128)S(1)} collective-permute-done((f32[18,34,1]{2,0,1:T(8,128)S(1)}, f32[18,34,1]{2,0,1:T(8,128)S(1)}, u32[]{:S(2)}, u32[]{:S(2)}) %collective-permute-start.29) | collective-permute-done | bytes 2480 | tf_op jit(solution)/shard_map/ppermute | solution.py:27
  165.9 2.1 collective-permute-start.30
  169.3 1.8 collective-permute-done.31
  171.1 1.9 collective-permute-start.32
  173.0 8.4 %collective-permute-start.33 = (f32[18,1,128]{2,0,1:T(8,128)S(1)}, f32[18,1,128]{2,0,1:T(8,128)S(1)}, u32[]{:S(2)}, u32[]{:S(2)}) collective-permute-start(f32[18,1,128]{2,0,1:T(8,128)S(1)} %get-tuple-element.467), channel_id=1, source_target_pairs={{2,0},{4,2},{6,4},{8,6},{10,8},{12,10},{14,12},{16,14},{18,16},{20... | collective-permute-start | bytes 27656 | tf_op jit(solution)/shard_map/ppermute | solution.py:27
  183.1 1.8 collective-permute-start.34
  186.1 8.5 %collective-permute-done.34 = f32[18,34,1]{2,0,1:T(8,128)S(1)} collective-permute-done((f32[18,34,1]{2,0,1:T(8,128)S(1)}, f32[18,34,1]{2,0,1:T(8,128)S(1)}, u32[]{:S(2)}, u32[]{:S(2)}) %collective-permute-start.34) | collective-permute-done | bytes 2480 | tf_op jit(solution)/shard_map/ppermute | solution.py:25
  194.7 4.5 %collective-permute-done.35 = f32[18,34,1]{2,0,1:T(8,128)S(1)} collective-permute-done((f32[18,34,1]{2,0,1:T(8,128)S(1)}, f32[18,34,1]{2,0,1:T(8,128)S(1)}, u32[]{:S(2)}, u32[]{:S(2)}) %collective-permute-start.35) | collective-permute-done | bytes 2480 | tf_op jit(solution)/shard_map/ppermute | solution.py:27
  201.1 1.9 collective-permute-start.36
  204.3 1.8 collective-permute-done.37
  206.1 1.9 collective-permute-start.38
  208.0 8.1 %collective-permute-start.39 = (f32[18,1,128]{2,0,1:T(8,128)S(1)}, f32[18,1,128]{2,0,1:T(8,128)S(1)}, u32[]{:S(2)}, u32[]{:S(2)}) collective-permute-start(f32[18,1,128]{2,0,1:T(8,128)S(1)} %get-tuple-element.465), channel_id=1, source_target_pairs={{2,0},{4,2},{6,4},{8,6},{10,8},{12,10},{14,12},{16,14},{18,16},{20... | collective-permute-start | bytes 27656 | tf_op jit(solution)/shard_map/ppermute | solution.py:27
  217.8 1.5 collective-permute-start.40
  220.6 8.6 %collective-permute-done.40 = f32[18,34,1]{2,0,1:T(8,128)S(1)} collective-permute-done((f32[18,34,1]{2,0,1:T(8,128)S(1)}, f32[18,34,1]{2,0,1:T(8,128)S(1)}, u32[]{:S(2)}, u32[]{:S(2)}) %collective-permute-start.40) | collective-permute-done | bytes 2480 | tf_op jit(solution)/shard_map/ppermute | solution.py:25
  229.2 4.3 %collective-permute-done.41 = f32[18,34,1]{2,0,1:T(8,128)S(1)} collective-permute-done((f32[18,34,1]{2,0,1:T(8,128)S(1)}, f32[18,34,1]{2,0,1:T(8,128)S(1)}, u32[]{:S(2)}, u32[]{:S(2)}) %collective-permute-start.41) | collective-permute-done | bytes 2480 | tf_op jit(solution)/shard_map/ppermute | solution.py:27
  234.5 1.7 subtract_multiply_fusion
  236.6 8.0 %all_to_all.8 = f32[16,32,128]{2,0,1:T(8,128)S(1)} all-to-all(f32[16,32,128]{2,0,1:T(8,128)S(1)} %fusion.145), channel_id=1, replica_groups=mesh['gx'=8,'gy'=16,'gz'=2] {'gz'}, dimensions={1} | all-to-all | bytes 524288 | tf_op jit(solution)/shard_map/all_to_all | solution.py:192
  244.6 3.4 %all-to-all-start = ((f32[16,32,128]{2,0,1:T(8,128)}), f32[16,32,128]{2,0,1:T(8,128)S(1)}, u32[]{:S(2)}, u32[]{:S(2)}) async-start(f32[16,32,128]{2,0,1:T(8,128)} %get-tuple-element.410), calls=%async_computation | async-start | bytes 524288 | tf_op jit(solution)/shard_map/all_to_all | solution.py:191
  248.2 5.0 %all-to-all-done = f32[16,32,128]{2,0,1:T(8,128)S(1)} async-done(((f32[16,32,128]{2,0,1:T(8,128)}), f32[16,32,128]{2,0,1:T(8,128)S(1)}, u32[]{:S(2)}, u32[]{:S(2)}) %all-to-all-start) | async-done | bytes 262176 | tf_op jit(solution)/shard_map/all_to_all | solution.py:191
  258.3 1.9 collective-permute-start.44
  260.3 7.2 %collective-permute-start.45 = (f32[2,18,1,256]{3,2,1,0:T(1,128)S(1)}, f32[2,18,1,256]{3,2,1,0:T(1,128)S(1)}, u32[]{:S(2)}, u32[]{:S(2)}) collective-permute-start(f32[2,18,1,256]{3,2,1,0:T(1,128)S(1)} %get-tuple-element.443), channel_id=1, source_target_pairs={{1,0},{2,1},{3,2},{4,3},{5,4},{6,5},{7,6},{8,7},{9,8},{10,9},{11,1... | collective-permute-start | bytes 110600 | tf_op jit(solution)/shard_map/ppermute | solution.py:27
  267.6 1.7 collective-permute-done.45
  269.4 27.3 %while.38 = (s32[]{:T(128)}, f32[16,16,256]{2,1,0:T(8,128)S(1)}, s32[16,16,256]{2,1,0:T(8,128)S(1)}, s32[]{:T(128)}, s32[8]{0:T(128)S(1)}, /*index=5*/s32[16,16,...) while((s32[]{:T(128)}, f32[16,16,256]{2,1,0:T(8,128)S(1)}, ...), condition=%wide.region_2.3_spmd, body=%wide.region_1.2_spmd.sunk | while | flops 19849228 | bytes 2048038 | solution.py:159
  299.4 1.8 collective-permute-done.47
  301.3 1.9 collective-permute-start.48
  303.2 7.2 %collective-permute-start.49 = (f32[2,18,1,256]{3,2,1,0:T(1,128)S(1)}, f32[2,18,1,256]{3,2,1,0:T(1,128)S(1)}, u32[]{:S(2)}, u32[]{:S(2)}) collective-permute-start(f32[2,18,1,256]{3,2,1,0:T(1,128)S(1)} %get-tuple-element.441), channel_id=1, source_target_pairs={{1,0},{2,1},{3,2},{4,3},{5,4},{6,5},{7,6},{8,7},{9,8},{10,9},{11,1... | collective-permute-start | bytes 110600 | tf_op jit(solution)/shard_map/ppermute | solution.py:27
  312.2 27.7 %while.39 = (s32[]{:T(128)}, f32[16,16,256]{2,1,0:T(8,128)S(1)}, s32[16,16,256]{2,1,0:T(8,128)S(1)}, s32[]{:T(128)}, s32[8]{0:T(128)S(1)}, /*index=5*/s32[16,16,...) while((s32[]{:T(128)}, f32[16,16,256]{2,1,0:T(8,128)S(1)}, ...), condition=%wide.region_4.5_spmd, body=%wide.region_3.4_spmd.sunk | while | flops 19849228 | bytes 2048038 | solution.py:159
  (311 shorter events, 74.6 us)
Async XLA Ops:
  2.3 8.7 %collective-permute-start = (f32[1,32,128]{2,0,1:T(1,128)S(1)}, f32[1,32,128]{2,0,1:T(1,128)S(1)}, u32[]{:S(2)}, u32[]{:S(2)}) collective-permute-start(f32[1,32,128]{2,0,1:T(1,128)S(1)} %get-tuple-element.490), channel_id=1, source_target_pairs={{0,32},{32,64},{64,96},{96,128},{128,160},{160,192},{192,224},{1,3... | collective-permute-start | bytes 49160 | tf_op jit(solution)/shard_map/ppermute | solution.py:25
  4.0 7.0 %collective-permute-start.1 = (f32[1,32,128]{2,0,1:T(1,128)S(1)}, f32[1,32,128]{2,0,1:T(1,128)S(1)}, u32[]{:S(2)}, u32[]{:S(2)}) collective-permute-start(f32[1,32,128]{2,0,1:T(1,128)S(1)} %get-tuple-element.491), channel_id=1, source_target_pairs={{32,0},{64,32},{96,64},{128,96},{160,128},{192,160},{224,192},{33,... | collective-permute-start | bytes 49160 | tf_op jit(solution)/shard_map/ppermute | solution.py:27
  5.4 15.7 %collective-permute-start.6 = (f32[1,32,128]{2,0,1:T(1,128)S(1)}, f32[1,32,128]{2,0,1:T(1,128)S(1)}, u32[]{:S(2)}, u32[]{:S(2)}) collective-permute-start(f32[1,32,128]{2,0,1:T(1,128)S(1)} %get-tuple-element.488), channel_id=1, source_target_pairs={{0,32},{32,64},{64,96},{96,128},{128,160},{160,192},{192,224},{1,3... | collective-permute-start | bytes 49160 | tf_op jit(solution)/shard_map/ppermute | solution.py:25
  9.7 11.4 %collective-permute-start.7 = (f32[1,32,128]{2,0,1:T(1,128)S(1)}, f32[1,32,128]{2,0,1:T(1,128)S(1)}, u32[]{:S(2)}, u32[]{:S(2)}) collective-permute-start(f32[1,32,128]{2,0,1:T(1,128)S(1)} %get-tuple-element.489), channel_id=1, source_target_pairs={{32,0},{64,32},{96,64},{128,96},{160,128},{192,160},{224,192},{33,... | collective-permute-start | bytes 49160 | tf_op jit(solution)/shard_map/ppermute | solution.py:27
  11.0 20.2 %collective-permute-start.2 = (f32[18,1,128]{2,0,1:T(8,128)S(1)}, f32[18,1,128]{2,0,1:T(8,128)S(1)}, u32[]{:S(2)}, u32[]{:S(2)}) collective-permute-start(f32[18,1,128]{2,0,1:T(8,128)S(1)} %get-tuple-element.476), channel_id=1, source_target_pairs={{0,2},{2,4},{4,6},{6,8},{8,10},{10,12},{12,14},{14,16},{16,18},{18... | collective-permute-start | bytes 27656 | tf_op jit(solution)/shard_map/ppermute | solution.py:25
  14.5 16.7 %collective-permute-start.3 = (f32[18,1,128]{2,0,1:T(8,128)S(1)}, f32[18,1,128]{2,0,1:T(8,128)S(1)}, u32[]{:S(2)}, u32[]{:S(2)}) collective-permute-start(f32[18,1,128]{2,0,1:T(8,128)S(1)} %get-tuple-element.477), channel_id=1, source_target_pairs={{2,0},{4,2},{6,4},{8,6},{10,8},{12,10},{14,12},{16,14},{18,16},{20... | collective-permute-start | bytes 27656 | tf_op jit(solution)/shard_map/ppermute | solution.py:27
  21.1 14.6 %collective-permute-start.8 = (f32[18,1,128]{2,0,1:T(8,128)S(1)}, f32[18,1,128]{2,0,1:T(8,128)S(1)}, u32[]{:S(2)}, u32[]{:S(2)}) collective-permute-start(f32[18,1,128]{2,0,1:T(8,128)S(1)} %get-tuple-element.474), channel_id=1, source_target_pairs={{0,2},{2,4},{4,6},{6,8},{8,10},{10,12},{12,14},{14,16},{16,18},{18... | collective-permute-start | bytes 27656 | tf_op jit(solution)/shard_map/ppermute | solution.py:25
  23.1 12.7 %collective-permute-start.9 = (f32[18,1,128]{2,0,1:T(8,128)S(1)}, f32[18,1,128]{2,0,1:T(8,128)S(1)}, u32[]{:S(2)}, u32[]{:S(2)}) collective-permute-start(f32[18,1,128]{2,0,1:T(8,128)S(1)} %get-tuple-element.475), channel_id=1, source_target_pairs={{2,0},{4,2},{6,4},{8,6},{10,8},{12,10},{14,12},{16,14},{18,16},{20... | collective-permute-start | bytes 27656 | tf_op jit(solution)/shard_map/ppermute | solution.py:27
  31.5 12.7 %collective-permute-start.4 = (f32[18,34,1]{2,0,1:T(8,128)S(1)}, f32[18,34,1]{2,0,1:T(8,128)S(1)}, u32[]{:S(2)}, u32[]{:S(2)}) collective-permute-start(f32[18,34,1]{2,0,1:T(8,128)S(1)} %get-tuple-element.462), channel_id=1, source_target_pairs={{0,1},{2,3},{4,5},{6,7},{8,9},{10,11},{12,13},{14,15},{16,17},{18,... | collective-permute-start | bytes 7352 | tf_op jit(solution)/shard_map/ppermute | solution.py:25
  34.5 14.4 %collective-permute-start.5 = (f32[18,34,1]{2,0,1:T(8,128)S(1)}, f32[18,34,1]{2,0,1:T(8,128)S(1)}, u32[]{:S(2)}, u32[]{:S(2)}) collective-permute-start(f32[18,34,1]{2,0,1:T(8,128)S(1)} %get-tuple-element.463), channel_id=1, source_target_pairs={{1,0},{3,2},{5,4},{7,6},{9,8},{11,10},{13,12},{15,14},{17,16},{19,... | collective-permute-start | bytes 7352 | tf_op jit(solution)/shard_map/ppermute | solution.py:27
  36.0 17.1 %collective-permute-start.10 = (f32[18,34,1]{2,0,1:T(8,128)S(1)}, f32[18,34,1]{2,0,1:T(8,128)S(1)}, u32[]{:S(2)}, u32[]{:S(2)}) collective-permute-start(f32[18,34,1]{2,0,1:T(8,128)S(1)} %get-tuple-element.460), channel_id=1, source_target_pairs={{0,1},{2,3},{4,5},{6,7},{8,9},{10,11},{12,13},{14,15},{16,17},{18,... | collective-permute-start | bytes 7352 | tf_op jit(solution)/shard_map/ppermute | solution.py:25
  40.6 17.2 %collective-permute-start.11 = (f32[18,34,1]{2,0,1:T(8,128)S(1)}, f32[18,34,1]{2,0,1:T(8,128)S(1)}, u32[]{:S(2)}, u32[]{:S(2)}) collective-permute-start(f32[18,34,1]{2,0,1:T(8,128)S(1)} %get-tuple-element.461), channel_id=1, source_target_pairs={{1,0},{3,2},{5,4},{7,6},{9,8},{11,10},{13,12},{15,14},{17,16},{19,... | collective-permute-start | bytes 7352 | tf_op jit(solution)/shard_map/ppermute | solution.py:27
  59.8 3.3 collective-permute-start.12
  61.8 4.1 %collective-permute-start.13 = (f32[1,32,128]{2,0,1:T(1,128)S(1)}, f32[1,32,128]{2,0,1:T(1,128)S(1)}, u32[]{:S(2)}, u32[]{:S(2)}) collective-permute-start(f32[1,32,128]{2,0,1:T(1,128)S(1)} %get-tuple-element.487), channel_id=1, source_target_pairs={{32,0},{64,32},{96,64},{128,96},{160,128},{192,160},{224,192},{33,... | collective-permute-start | bytes 49160 | tf_op jit(solution)/shard_map/ppermute | solution.py:27
  65.9 10.1 %collective-permute-start.14 = (f32[18,1,128]{2,0,1:T(8,128)S(1)}, f32[18,1,128]{2,0,1:T(8,128)S(1)}, u32[]{:S(2)}, u32[]{:S(2)}) collective-permute-start(f32[18,1,128]{2,0,1:T(8,128)S(1)} %get-tuple-element.472), channel_id=1, source_target_pairs={{0,2},{2,4},{4,6},{6,8},{8,10},{10,12},{12,14},{14,16},{16,18},{18... | collective-permute-start | bytes 27656 | tf_op jit(solution)/shard_map/ppermute | solution.py:25
  67.8 9.5 %collective-permute-start.15 = (f32[18,1,128]{2,0,1:T(8,128)S(1)}, f32[18,1,128]{2,0,1:T(8,128)S(1)}, u32[]{:S(2)}, u32[]{:S(2)}) collective-permute-start(f32[18,1,128]{2,0,1:T(8,128)S(1)} %get-tuple-element.473), channel_id=1, source_target_pairs={{2,0},{4,2},{6,4},{8,6},{10,8},{12,10},{14,12},{16,14},{18,16},{20... | collective-permute-start | bytes 27656 | tf_op jit(solution)/shard_map/ppermute | solution.py:27
  77.6 11.0 %collective-permute-start.16 = (f32[18,34,1]{2,0,1:T(8,128)S(1)}, f32[18,34,1]{2,0,1:T(8,128)S(1)}, u32[]{:S(2)}, u32[]{:S(2)}) collective-permute-start(f32[18,34,1]{2,0,1:T(8,128)S(1)} %get-tuple-element.458), channel_id=1, source_target_pairs={{0,1},{2,3},{4,5},{6,7},{8,9},{10,11},{12,13},{14,15},{16,17},{18,... | collective-permute-start | bytes 7352 | tf_op jit(solution)/shard_map/ppermute | solution.py:25
  79.1 14.2 %collective-permute-start.17 = (f32[18,34,1]{2,0,1:T(8,128)S(1)}, f32[18,34,1]{2,0,1:T(8,128)S(1)}, u32[]{:S(2)}, u32[]{:S(2)}) collective-permute-start(f32[18,34,1]{2,0,1:T(8,128)S(1)} %get-tuple-element.459), channel_id=1, source_target_pairs={{1,0},{3,2},{5,4},{7,6},{9,8},{11,10},{13,12},{15,14},{17,16},{19,... | collective-permute-start | bytes 7352 | tf_op jit(solution)/shard_map/ppermute | solution.py:27
  95.2 3.3 collective-permute-start.18
  97.2 4.2 %collective-permute-start.19 = (f32[1,32,128]{2,0,1:T(1,128)S(1)}, f32[1,32,128]{2,0,1:T(1,128)S(1)}, u32[]{:S(2)}, u32[]{:S(2)}) collective-permute-start(f32[1,32,128]{2,0,1:T(1,128)S(1)} %get-tuple-element.485), channel_id=1, source_target_pairs={{32,0},{64,32},{96,64},{128,96},{160,128},{192,160},{224,192},{33,... | collective-permute-start | bytes 49160 | tf_op jit(solution)/shard_map/ppermute | solution.py:27
  101.5 10.4 %collective-permute-start.20 = (f32[18,1,128]{2,0,1:T(8,128)S(1)}, f32[18,1,128]{2,0,1:T(8,128)S(1)}, u32[]{:S(2)}, u32[]{:S(2)}) collective-permute-start(f32[18,1,128]{2,0,1:T(8,128)S(1)} %get-tuple-element.470), channel_id=1, source_target_pairs={{0,2},{2,4},{4,6},{6,8},{8,10},{10,12},{12,14},{14,16},{16,18},{18... | collective-permute-start | bytes 27656 | tf_op jit(solution)/shard_map/ppermute | solution.py:25
  103.4 9.8 %collective-permute-start.21 = (f32[18,1,128]{2,0,1:T(8,128)S(1)}, f32[18,1,128]{2,0,1:T(8,128)S(1)}, u32[]{:S(2)}, u32[]{:S(2)}) collective-permute-start(f32[18,1,128]{2,0,1:T(8,128)S(1)} %get-tuple-element.471), channel_id=1, source_target_pairs={{2,0},{4,2},{6,4},{8,6},{10,8},{12,10},{14,12},{16,14},{18,16},{20... | collective-permute-start | bytes 27656 | tf_op jit(solution)/shard_map/ppermute | solution.py:27
  113.5 10.7 %collective-permute-start.22 = (f32[18,34,1]{2,0,1:T(8,128)S(1)}, f32[18,34,1]{2,0,1:T(8,128)S(1)}, u32[]{:S(2)}, u32[]{:S(2)}) collective-permute-start(f32[18,34,1]{2,0,1:T(8,128)S(1)} %get-tuple-element.456), channel_id=1, source_target_pairs={{0,1},{2,3},{4,5},{6,7},{8,9},{10,11},{12,13},{14,15},{16,17},{18,... | collective-permute-start | bytes 7352 | tf_op jit(solution)/shard_map/ppermute | solution.py:25
  115.0 14.0 %collective-permute-start.23 = (f32[18,34,1]{2,0,1:T(8,128)S(1)}, f32[18,34,1]{2,0,1:T(8,128)S(1)}, u32[]{:S(2)}, u32[]{:S(2)}) collective-permute-start(f32[18,34,1]{2,0,1:T(8,128)S(1)} %get-tuple-element.457), channel_id=1, source_target_pairs={{1,0},{3,2},{5,4},{7,6},{9,8},{11,10},{13,12},{15,14},{17,16},{19,... | collective-permute-start | bytes 7352 | tf_op jit(solution)/shard_map/ppermute | solution.py:27
  130.9 3.5 %collective-permute-start.24 = (f32[1,32,128]{2,0,1:T(1,128)S(1)}, f32[1,32,128]{2,0,1:T(1,128)S(1)}, u32[]{:S(2)}, u32[]{:S(2)}) collective-permute-start(f32[1,32,128]{2,0,1:T(1,128)S(1)} %get-tuple-element.482), channel_id=1, source_target_pairs={{0,32},{32,64},{64,96},{96,128},{128,160},{160,192},{192,224},{1,3... | collective-permute-start | bytes 49160 | tf_op jit(solution)/shard_map/ppermute | solution.py:25
  133.0 3.6 %collective-permute-start.25 = (f32[1,32,128]{2,0,1:T(1,128)S(1)}, f32[1,32,128]{2,0,1:T(1,128)S(1)}, u32[]{:S(2)}, u32[]{:S(2)}) collective-permute-start(f32[1,32,128]{2,0,1:T(1,128)S(1)} %get-tuple-element.483), channel_id=1, source_target_pairs={{32,0},{64,32},{96,64},{128,96},{160,128},{192,160},{224,192},{33,... | collective-permute-start | bytes 49160 | tf_op jit(solution)/shard_map/ppermute | solution.py:27
  136.6 10.2 %collective-permute-start.26 = (f32[18,1,128]{2,0,1:T(8,128)S(1)}, f32[18,1,128]{2,0,1:T(8,128)S(1)}, u32[]{:S(2)}, u32[]{:S(2)}) collective-permute-start(f32[18,1,128]{2,0,1:T(8,128)S(1)} %get-tuple-element.468), channel_id=1, source_target_pairs={{0,2},{2,4},{4,6},{6,8},{8,10},{10,12},{12,14},{14,16},{16,18},{18... | collective-permute-start | bytes 27656 | tf_op jit(solution)/shard_map/ppermute | solution.py:25
  138.5 9.6 %collective-permute-start.27 = (f32[18,1,128]{2,0,1:T(8,128)S(1)}, f32[18,1,128]{2,0,1:T(8,128)S(1)}, u32[]{:S(2)}, u32[]{:S(2)}) collective-permute-start(f32[18,1,128]{2,0,1:T(8,128)S(1)} %get-tuple-element.469), channel_id=1, source_target_pairs={{2,0},{4,2},{6,4},{8,6},{10,8},{12,10},{14,12},{16,14},{18,16},{20... | collective-permute-start | bytes 27656 | tf_op jit(solution)/shard_map/ppermute | solution.py:27
  148.4 10.8 %collective-permute-start.28 = (f32[18,34,1]{2,0,1:T(8,128)S(1)}, f32[18,34,1]{2,0,1:T(8,128)S(1)}, u32[]{:S(2)}, u32[]{:S(2)}) collective-permute-start(f32[18,34,1]{2,0,1:T(8,128)S(1)} %get-tuple-element.454), channel_id=1, source_target_pairs={{0,1},{2,3},{4,5},{6,7},{8,9},{10,11},{12,13},{14,15},{16,17},{18,... | collective-permute-start | bytes 7352 | tf_op jit(solution)/shard_map/ppermute | solution.py:25
  149.9 14.0 %collective-permute-start.29 = (f32[18,34,1]{2,0,1:T(8,128)S(1)}, f32[18,34,1]{2,0,1:T(8,128)S(1)}, u32[]{:S(2)}, u32[]{:S(2)}) collective-permute-start(f32[18,34,1]{2,0,1:T(8,128)S(1)} %get-tuple-element.455), channel_id=1, source_target_pairs={{1,0},{3,2},{5,4},{7,6},{9,8},{11,10},{13,12},{15,14},{17,16},{19,... | collective-permute-start | bytes 7352 | tf_op jit(solution)/shard_map/ppermute | solution.py:27
  165.9 3.4 %collective-permute-start.30 = (f32[1,32,128]{2,0,1:T(1,128)S(1)}, f32[1,32,128]{2,0,1:T(1,128)S(1)}, u32[]{:S(2)}, u32[]{:S(2)}) collective-permute-start(f32[1,32,128]{2,0,1:T(1,128)S(1)} %get-tuple-element.480), channel_id=1, source_target_pairs={{0,32},{32,64},{64,96},{96,128},{128,160},{160,192},{192,224},{1,3... | collective-permute-start | bytes 49160 | tf_op jit(solution)/shard_map/ppermute | solution.py:25
  168.0 3.1 collective-permute-start.31
  171.1 10.4 %collective-permute-start.32 = (f32[18,1,128]{2,0,1:T(8,128)S(1)}, f32[18,1,128]{2,0,1:T(8,128)S(1)}, u32[]{:S(2)}, u32[]{:S(2)}) collective-permute-start(f32[18,1,128]{2,0,1:T(8,128)S(1)} %get-tuple-element.466), channel_id=1, source_target_pairs={{0,2},{2,4},{4,6},{6,8},{8,10},{10,12},{12,14},{14,16},{16,18},{18... | collective-permute-start | bytes 27656 | tf_op jit(solution)/shard_map/ppermute | solution.py:25
  173.0 9.8 %collective-permute-start.33 = (f32[18,1,128]{2,0,1:T(8,128)S(1)}, f32[18,1,128]{2,0,1:T(8,128)S(1)}, u32[]{:S(2)}, u32[]{:S(2)}) collective-permute-start(f32[18,1,128]{2,0,1:T(8,128)S(1)} %get-tuple-element.467), channel_id=1, source_target_pairs={{2,0},{4,2},{6,4},{8,6},{10,8},{12,10},{14,12},{16,14},{18,16},{20... | collective-permute-start | bytes 27656 | tf_op jit(solution)/shard_map/ppermute | solution.py:27
  183.1 11.6 %collective-permute-start.34 = (f32[18,34,1]{2,0,1:T(8,128)S(1)}, f32[18,34,1]{2,0,1:T(8,128)S(1)}, u32[]{:S(2)}, u32[]{:S(2)}) collective-permute-start(f32[18,34,1]{2,0,1:T(8,128)S(1)} %get-tuple-element.452), channel_id=1, source_target_pairs={{0,1},{2,3},{4,5},{6,7},{8,9},{10,11},{12,13},{14,15},{16,17},{18,... | collective-permute-start | bytes 7352 | tf_op jit(solution)/shard_map/ppermute | solution.py:25
  184.8 14.3 %collective-permute-start.35 = (f32[18,34,1]{2,0,1:T(8,128)S(1)}, f32[18,34,1]{2,0,1:T(8,128)S(1)}, u32[]{:S(2)}, u32[]{:S(2)}) collective-permute-start(f32[18,34,1]{2,0,1:T(8,128)S(1)} %get-tuple-element.453), channel_id=1, source_target_pairs={{1,0},{3,2},{5,4},{7,6},{9,8},{11,10},{13,12},{15,14},{17,16},{19,... | collective-permute-start | bytes 7352 | tf_op jit(solution)/shard_map/ppermute | solution.py:27
  201.1 3.2 collective-permute-start.36
  203.0 3.1 collective-permute-start.37
  206.1 10.1 %collective-permute-start.38 = (f32[18,1,128]{2,0,1:T(8,128)S(1)}, f32[18,1,128]{2,0,1:T(8,128)S(1)}, u32[]{:S(2)}, u32[]{:S(2)}) collective-permute-start(f32[18,1,128]{2,0,1:T(8,128)S(1)} %get-tuple-element.464), channel_id=1, source_target_pairs={{0,2},{2,4},{4,6},{6,8},{8,10},{10,12},{12,14},{14,16},{16,18},{18... | collective-permute-start | bytes 27656 | tf_op jit(solution)/shard_map/ppermute | solution.py:25
  208.0 9.5 %collective-permute-start.39 = (f32[18,1,128]{2,0,1:T(8,128)S(1)}, f32[18,1,128]{2,0,1:T(8,128)S(1)}, u32[]{:S(2)}, u32[]{:S(2)}) collective-permute-start(f32[18,1,128]{2,0,1:T(8,128)S(1)} %get-tuple-element.465), channel_id=1, source_target_pairs={{2,0},{4,2},{6,4},{8,6},{10,8},{12,10},{14,12},{16,14},{18,16},{20... | collective-permute-start | bytes 27656 | tf_op jit(solution)/shard_map/ppermute | solution.py:27
  217.8 11.4 %collective-permute-start.40 = (f32[18,34,1]{2,0,1:T(8,128)S(1)}, f32[18,34,1]{2,0,1:T(8,128)S(1)}, u32[]{:S(2)}, u32[]{:S(2)}) collective-permute-start(f32[18,34,1]{2,0,1:T(8,128)S(1)} %get-tuple-element.450), channel_id=1, source_target_pairs={{0,1},{2,3},{4,5},{6,7},{8,9},{10,11},{12,13},{14,15},{16,17},{18,... | collective-permute-start | bytes 7352 | tf_op jit(solution)/shard_map/ppermute | solution.py:25
  219.3 14.2 %collective-permute-start.41 = (f32[18,34,1]{2,0,1:T(8,128)S(1)}, f32[18,34,1]{2,0,1:T(8,128)S(1)}, u32[]{:S(2)}, u32[]{:S(2)}) collective-permute-start(f32[18,34,1]{2,0,1:T(8,128)S(1)} %get-tuple-element.451), channel_id=1, source_target_pairs={{1,0},{3,2},{5,4},{7,6},{9,8},{11,10},{13,12},{15,14},{17,16},{19,... | collective-permute-start | bytes 7352 | tf_op jit(solution)/shard_map/ppermute | solution.py:27
  236.6 11.5 %copy-start.5 = (f32[3,64]{1,0:T(4,128)S(1)}, f32[3,64]{1,0:T(4,128)}, u32[]{:S(2)}) copy-start(f32[3,64]{1,0:T(4,128)} %param.21) | copy-start | bytes 2308
  236.6 11.6 %copy-start.1 = (s32[2,16,16,256]{3,2,1,0:T(8,128)S(1)}, s32[2,16,16,256]{3,2,1,0:T(8,128)}, u32[]{:S(2)}) copy-start(s32[2,16,16,256]{3,2,1,0:T(8,128)} %param.19) | copy-start | bytes 1572868
  244.6 8.6 %all-to-all-start = ((f32[16,32,128]{2,0,1:T(8,128)}), f32[16,32,128]{2,0,1:T(8,128)S(1)}, u32[]{:S(2)}, u32[]{:S(2)}) async-start(f32[16,32,128]{2,0,1:T(8,128)} %get-tuple-element.410), calls=%async_computation | async-start | bytes 524288 | tf_op jit(solution)/shard_map/all_to_all | solution.py:191
  248.2 5.5 %copy-start.2 = (s32[16,16,256]{2,1,0:T(8,128)S(1)}, s32[16,16,256]{2,1,0:T(8,128)}, u32[]{:S(2)}) copy-start(s32[16,16,256]{2,1,0:T(8,128)} %param.16) | copy-start | bytes 786436
  248.2 5.5 %copy-start.3 = (s32[16,16,256]{2,1,0:T(8,128)S(1)}, s32[16,16,256]{2,1,0:T(8,128)}, u32[]{:S(2)}) copy-start(s32[16,16,256]{2,1,0:T(8,128)} %param.18) | copy-start | bytes 786436
  248.2 5.5 %copy-start.4 = (s32[16,16,256]{2,1,0:T(8,128)S(1)}, s32[16,16,256]{2,1,0:T(8,128)}, u32[]{:S(2)}) copy-start(s32[16,16,256]{2,1,0:T(8,128)} %param.17) | copy-start | bytes 786436
  253.8 2.7 copy-start.6
  253.9 3.2 collective-permute-start.42
  255.2 3.1 collective-permute-start.43
  258.3 9.3 %collective-permute-start.44 = (f32[2,18,1,256]{3,2,1,0:T(1,128)S(1)}, f32[2,18,1,256]{3,2,1,0:T(1,128)S(1)}, u32[]{:S(2)}, u32[]{:S(2)}) collective-permute-start(f32[2,18,1,256]{3,2,1,0:T(1,128)S(1)} %get-tuple-element.442), channel_id=1, source_target_pairs={{0,1},{1,2},{2,3},{3,4},{4,5},{5,6},{6,7},{7,8},{8,9},{9,10},{10,1... | collective-permute-start | bytes 110600 | tf_op jit(solution)/shard_map/ppermute | solution.py:25
  260.3 9.0 %collective-permute-start.45 = (f32[2,18,1,256]{3,2,1,0:T(1,128)S(1)}, f32[2,18,1,256]{3,2,1,0:T(1,128)S(1)}, u32[]{:S(2)}, u32[]{:S(2)}) collective-permute-start(f32[2,18,1,256]{3,2,1,0:T(1,128)S(1)} %get-tuple-element.443), channel_id=1, source_target_pairs={{1,0},{2,1},{3,2},{4,3},{5,4},{6,5},{7,6},{8,7},{9,8},{10,9},{11,1... | collective-permute-start | bytes 110600 | tf_op jit(solution)/shard_map/ppermute | solution.py:27
  296.8 2.6 collective-permute-start.46
  298.1 3.1 collective-permute-start.47
  301.3 10.0 %collective-permute-start.48 = (f32[2,18,1,256]{3,2,1,0:T(1,128)S(1)}, f32[2,18,1,256]{3,2,1,0:T(1,128)S(1)}, u32[]{:S(2)}, u32[]{:S(2)}) collective-permute-start(f32[2,18,1,256]{3,2,1,0:T(1,128)S(1)} %get-tuple-element.440), channel_id=1, source_target_pairs={{0,1},{1,2},{2,3},{3,4},{4,5},{5,6},{6,7},{7,8},{8,9},{9,10},{10,1... | collective-permute-start | bytes 110600 | tf_op jit(solution)/shard_map/ppermute | solution.py:25
  303.2 8.9 %collective-permute-start.49 = (f32[2,18,1,256]{3,2,1,0:T(1,128)S(1)}, f32[2,18,1,256]{3,2,1,0:T(1,128)S(1)}, u32[]{:S(2)}, u32[]{:S(2)}) collective-permute-start(f32[2,18,1,256]{3,2,1,0:T(1,128)S(1)} %get-tuple-element.441), channel_id=1, source_target_pairs={{1,0},{2,1},{3,2},{4,3},{5,4},{6,5},{7,6},{8,7},{9,8},{10,9},{11,1... | collective-permute-start | bytes 110600 | tf_op jit(solution)/shard_map/ppermute | solution.py:27
  340.0 0.9 copy-start
where the time goes:
time: 345 us; the launch traced here: 341 us
  starting transfers between devices  148 us (43%)
  waiting for transfers between devices  109 us (32%)
  loops' own time  23.6 us (7%)
  other arithmetic  20 us (6%)
  local copies, waits for them, and re-layouts  19.3 us (6%)
  matrix products  11.9 us (3%)
  blocking collectives  8.02 us (2%)
    ppermute x25, starting transfers between devices, extended(): lax.ppermute(head, axis, [((i + 1) % count, i) for i in range(ends)])  91.4 us
    ppermute x25, waiting for transfers between devices, extended(): lax.ppermute(head, axis, [((i + 1) % count, i) for i in range(ends)])  56 us
    ppermute x25, starting transfers between devices, extended(): lax.ppermute(tail, axis, [(i, (i + 1) % count) for i in range(ends)])  52.9 us
    ppermute x25, waiting for transfers between devices, extended(): lax.ppermute(tail, axis, [(i, (i + 1) % count) for i in range(ends)])  47.7 us
    another operation x2, loops' own time, sweep_listed(): return lax.fori_loop(0, live_count, visit_tile, (envelope, label))  23.6 us
    dot_general x16, matrix products, one_piece(): jnp.dot(reach, onehot, precision=lax.Precision.HIGHEST, preferred_element...  11.9 us
    dynamic_slice x16, local copies, waits for them, and re-layouts, visit_tile(): start_row = listed[visit_index] * rows_tile  9.92 us
    all_to_all x1, blocking collectives, body(): lax.all_to_all(liquid_time, 'gz', split_axis=1, concat_axis=2, tiled=True)  8.02 us
  transfers between devices with their start and end apart: 51, of which 29 were waited for; matrix products, arithmetic and copies ran while one was open for 1% of the time, Pallas kernels for 0%

commit v1 on v0

v1 whole, which is shorter than its diff:
```python
import functools

import jax
import jax.numpy as jnp
from jax import lax
from jax.experimental import pallas as pl
from jax.experimental.pallas import tpu as pltpu
from jax.sharding import PartitionSpec as P

MESH = pl.DeviceIdType.MESH
D = 6
NX, NY, NZ = 16, 32, 128
EX = NX + 2 * D
OY = 8
EY = NY + 2 * OY
PITCH = 3 * D
GR = 16
GX = NX + 4
GY = GR + 16
TINY = 1e-30


def lanes(shape):
    return lax.broadcasted_iota(jnp.int32, shape, 1)


def rows(shape):
    return lax.broadcasted_iota(jnp.int32, shape, 0)


def clip03(heat):
    return jnp.minimum(jnp.maximum(heat, 0.0), 3.0)


def state(heat, base):
    solid = clip03(heat)
    return heat - solid * (2.0 / 3.0), base * (1.0 + solid * (1.0 / 6.0))


def face(temp, cond, temp_next, cond_next):
    total = jnp.maximum(cond + cond_next, TINY)
    return (cond * cond_next) * pltpu.reciprocal(total, approx=True) * (temp_next - temp)


def roll(value, amount, axis):
    return pltpu.roll(value, amount % value.shape[axis], axis)


class Main:
    def __init__(self):
        self.lane_end = lanes((EY, NZ)) == NZ - 1

    def up(self, v):
        return roll(v, -1, 0)

    def down(self, v):
        return roll(v, 1, 0)

    def edge(self, flux):
        return jnp.where(self.lane_end, 0.0, flux)


class Strip:
    def __init__(self):
        self.first = rows((8, NZ)) == 0
        self.last = rows((8, NZ)) == 7

    def up(self, v):
        turned = roll(v, -1, 0)
        return jnp.where(self.last, roll(turned, -PITCH, 1), turned)

    def down(self, v):
        turned = roll(v, 1, 0)
        return jnp.where(self.first, roll(turned, PITCH, 1), turned)

    def edge(self, flux):
        return flux


def substep(src, dst, base, step, form, finish=None):
    first, stop = step, EX - step
    before_t, before_k = state(src[first - 1], base[first - 1])
    here_t, here_k = state(src[first], base[first])
    into = face(before_t, before_k, here_t, here_k)

    def slab(x, carry):
        here_t, here_k, into = carry
        next_t, next_k = state(src[x + 1], base[x + 1])
        out_of = face(here_t, here_k, next_t, next_k)
        along_y = face(here_t, here_k, form.up(here_t), form.up(here_k))
        along_z = form.edge(face(here_t, here_k, roll(here_t, -1, 1), roll(here_k, -1, 1)))
        total = (out_of - into) + (along_y - form.down(along_y)) + (along_z - roll(along_z, 1, 1))
        heat = src[x] + 0.2 * total
        if finish is None:
            dst[x] = heat
        else:
            finish(x, here_t, heat)
        return next_t, next_k, out_of

    def pair(i, carry):
        x = first + 2 * i
        return slab(x + 1, slab(x, carry))

    lax.fori_loop(0, (stop - first) // 2, pair, (here_t, here_k, into))


def outcome(history, x, temp_before, heat):
    solid = clip03(heat)
    temp = heat - solid * (2.0 / 3.0)
    liquid = solid
    for s in range(1, 6):
        liquid = liquid + clip03(history[s, x])
    cooling = (temp_before - temp) * 10.0
    under = jnp.maximum(cooling, 0.0) * (0.5 + liquid * (0.1 / 3.0))
    return temp, under * under


def shift_z(low, high):
    lane = lanes(low.shape)
    low_down, high_down = roll(low, 1, 1), roll(high, 1, 1)
    low_up, high_up = roll(low, -1, 1), roll(high, -1, 1)
    zero = jnp.zeros_like(low)
    down = (jnp.where(lane == 0, zero, low_down), jnp.where(lane == 0, low_down, high_down))
    up = (jnp.where(lane == NZ - 1, high_up, low_up), jnp.where(lane == NZ - 1, zero, high_up))
    return down, up


def pick(ref, x, codes):
    here = (ref[0, x], ref[1, x])
    down, up = shift_z(*here)
    picked = []
    for half in range(2):
        code = codes[half]
        views = (
            ref[half, x - 1],
            ref[half, x + 1],
            roll(here[half], 1, 0),
            roll(here[half], -1, 0),
            down[half],
            up[half],
        )
        value = jnp.zeros_like(here[half])
        for number, view in enumerate(views):
            value = jnp.where(code == number + 1, view, value)
        picked.append(value)
    return picked


def reach_rows(turns):
    cos_a, sin_a = jnp.cos(turns[0:1]), jnp.sin(turns[0:1])
    cos_b, sin_b = jnp.cos(turns[1:2]), jnp.sin(turns[1:2])
    cos_c, sin_c = jnp.cos(turns[2:3]), jnp.sin(turns[2:3])
    row_x = (
        jnp.abs(cos_a * cos_c - sin_a * sin_c * cos_b)
        + jnp.abs(-cos_a * sin_c - sin_a * cos_c * cos_b)
        + jnp.abs(sin_a * sin_b)
    )
    row_y = (
        jnp.abs(sin_a * cos_c + cos_a * sin_c * cos_b)
        + jnp.abs(-sin_a * sin_c + cos_a * cos_c * cos_b)
        + jnp.abs(-cos_a * sin_b)
    )
    row_z = jnp.abs(sin_c * sin_b) + jnp.abs(cos_c * sin_b) + jnp.abs(cos_b)
    return row_x, row_y, row_z


def lookup(tables, side, code):
    pose = side & 63
    axis = jnp.maximum(code - 1, 0) >> 1
    parts = []
    for tile in range(side.shape[0] // 8):
        cut = slice(8 * tile, 8 * tile + 8)
        index = pose[cut] + ((axis[cut] & 1) << 6)
        xy = jnp.take_along_axis(tables[0], index, axis=1, mode="promise_in_bounds")
        z = jnp.take_along_axis(tables[1], index, axis=1, mode="promise_in_bounds")
        parts.append(jnp.where(axis[cut] == 2, z, xy))
    return jnp.concatenate(parts, axis=0)


def kernel(
    kelvin, conductance, melted, germ, nucleus, pose, captured, roster, turns,
    temp_out, env_out, grain_out,
    bricks, history, strip_h, strip_b, strip_out, strip_in, speed,
    strip_t, strip_s, lab, lab1, reach1, reach2, gspeed, grown, grown1, env1,
    heat_send, heat_recv, strip_send, strip_recv,
    speed_send, speed_recv_a, speed_recv_b, local_sem, lab_send, lab_recv,
):
    gx, gy, gz = (lax.axis_index(a) for a in ("gx", "gy", "gz"))
    ngx, ngy = lax.axis_size("gx"), lax.axis_size("gy")

    def at(dx, dy, z):
        return (lax.rem(gx + dx + ngx, ngx), lax.rem(gy + dy + ngy, ngy), z)

    other = 1 - gz
    cross = 2 * gz - 1
    xy = [(dx, dy) for dx in (-1, 0, 1) for dy in (-1, 0, 1) if (dx, dy) != (0, 0)]
    greeted = [at(dx, dy, gz) for dx, dy in xy]
    greeted += [at(dx, 0, other) for dx in (-1, 0, 1)]
    greeted += [at(dx, cross, other) for dx in (-1, 0, 1)]
    barrier = pltpu.get_barrier_semaphore()
    for device in greeted:
        pl.semaphore_signal(barrier, inc=1, device_id=device, device_id_type=MESH)

    def send(src, dst, send_sem, recv_sem, device):
        copy = pltpu.make_async_remote_copy(
            src_ref=src, dst_ref=dst, send_sem=send_sem, recv_sem=recv_sem,
            device_id=device, device_id_type=MESH,
        )
        copy.start()
        return copy

    own_rows = pl.ds(OY, NY)

    def opening(x, _):
        melt = melted[x].astype(jnp.float32)
        start = kelvin[x] + 1.5 * melt
        bricks[0, D + x, own_rows] = start + 2.0 * jnp.clip(start, 0.0, 1.0)
        bricks[1, D + x, own_rows] = conductance[x] * (0.25 + 0.75 * melt)
        return 0

    lax.fori_loop(0, NX, opening, 0)

    tiles = [roster[0, 0, i] for i in range(8)]

    def seeds(x, _):
        tile = x // 2
        active = tiles[0] == tile
        for number in tiles[1:]:
            active = jnp.logical_or(active, number == tile)
        for half in range(2):
            cut = pl.ds(half * NZ, NZ)
            label = germ[x, :, cut] * (nucleus[x, :, cut] * 64 + pose[x, :, cut])
            lab[0, half, 2 + x, pl.ds(8, GR)] = label
            for g in range(2):
                lab[1 + g, half, 2 + x, pl.ds(8, GR)] = jnp.where(
                    active, captured[g, x, :, cut], -1
                )
        return 0

    lax.fori_loop(0, NX, seeds, 0)

    pl.semaphore_wait(barrier, len(greeted))

    copies = []
    for i, (dx, dy) in enumerate(xy):
        deep = D if dx == 0 or dy == 0 else D - 1
        src_x = {-1: (D, deep), 0: (D, NX), 1: (D + NX - deep, deep)}[dx]
        dst_x = {-1: D + NX, 0: D, 1: D - deep}[dx]
        src_y = {-1: (OY, deep), 0: (OY, NY), 1: (OY + NY - deep, deep)}[dy]
        dst_y = {-1: OY + NY, 0: OY, 1: OY - deep}[dy]
        copies.append(send(
            bricks.at[:, pl.ds(*src_x), pl.ds(*src_y)],
            bricks.at[:, pl.ds(dst_x, src_x[1]), pl.ds(dst_y, src_y[1])],
            heat_send.at[i], heat_recv.at[i], at(dx, dy, gz),
        ))

    lab_copies = []
    for i, (dx, dg) in enumerate(xy):
        deep = 2 if dx == 0 or dg == 0 else 1
        src_x = {-1: (2, deep), 0: (2, NX), 1: (2 + NX - deep, deep)}[dx]
        dst_x = {-1: 2 + NX, 0: 2, 1: 2 - deep}[dx]
        src_y = {-1: (8, deep), 0: (8, GR), 1: (8 + GR - deep, deep)}[dg]
        dst_y = {-1: 8 + GR, 0: 8, 1: 8 - deep}[dg]
        if dg == 0:
            device = at(dx, 0, gz)
        elif dg == 1:
            device = at(dx, gz, other)
        else:
            device = at(dx, gz - 1, other)
        lab_copies.append(send(
            lab.at[pl.ds(0, 2), :, pl.ds(*src_x), pl.ds(*src_y)],
            lab.at[pl.ds(0, 2), :, pl.ds(dst_x, src_x[1]), pl.ds(dst_y, src_y[1])],
            lab_send.at[i], lab_recv.at[i], device,
        ))

    row_x, row_y, row_z = reach_rows(turns[...])
    tables = [
        jnp.broadcast_to(jnp.concatenate(pair, axis=1), (8, NZ))
        for pair in ((row_x, row_y), (row_z, row_z))
    ]

    for copy in copies:
        copy.wait()

    lane8 = lanes((8, NZ))
    row_all = rows((EY, NZ))
    outside_y = ((row_all < OY) & (gy == 0)) | ((row_all >= OY + NY) & (gy == ngy - 1))
    slot = lane8
    for tile in range(1, EY // 8):
        slot = jnp.where(lane8 >= tile * PITCH, lane8 - tile * PITCH, slot)
    in_use = lane8 < PITCH * (EY // 8)
    own_slot = (slot >= D * gz) & (slot < D * gz + 2 * D)
    halo_slot = jnp.logical_not(own_slot) & in_use
    turn = D * (1 - 2 * gz)

    def pack(x, _):
        outside_x = ((x < D) & (gx == 0)) | ((x >= D + NX) & (gx == ngx - 1))
        base = jnp.where(outside_x | outside_y, 0.0, bricks[1, x])
        bricks[1, x] = base
        heat = bricks[0, x]
        history[0, x] = heat
        packed = []
        for value in (heat, base):
            strip = jnp.zeros((8, NZ), jnp.float32)
            for tile in range(EY // 8):
                moved = pltpu.roll(
                    value[8 * tile : 8 * tile + 8], (PITCH * tile + 2 * D - D * gz) % NZ, 1
                )
                mine = own_slot & (lane8 >= tile * PITCH) & (lane8 < (tile + 1) * PITCH)
                strip = jnp.where(mine, moved, strip)
            packed.append(strip)
        strip_h[0, x] = packed[0]
        strip_b[x] = packed[1]
        strip_out[x] = jnp.where(halo_slot, pltpu.roll(packed[1], (turn + NZ) % NZ, 1), packed[0])
        return 0

    lax.fori_loop(0, EX, pack, 0)
    strip_copy = send(
        strip_out, strip_in, strip_send, strip_recv, at(0, 0, other)
    )

    main = Main()
    for step in range(1, 6):
        substep(
            history.at[step - 1], history.at[step], bricks.at[1], step, main
        )

    strip_copy.wait()

    def unpack(x, _):
        got = strip_in[x]
        strip_h[0, x] = jnp.where(halo_slot, pltpu.roll(got, (turn + NZ) % NZ, 1), strip_h[0, x])
        strip_b[x] = jnp.where(halo_slot, pltpu.roll(got, (2 * turn + NZ) % NZ, 1), strip_b[x])
        return 0

    lax.fori_loop(0, EX, unpack, 0)
    form = Strip()
    for step in range(1, 6):
        substep(strip_h.at[step - 1], strip_h.at[step], strip_b, step, form)

    def strip_end(x, temp_before, heat):
        strip_t[x - D], strip_s[x - D] = outcome(strip_h, x, temp_before, heat)

    substep(strip_h.at[5], None, strip_b, 6, form, strip_end)

    near = jnp.where(gz == 0, lane8 - (NZ - D), D - 1 - lane8) >= 0

    def brick_end(x, temp_before, heat):
        temp, fast = outcome(history, x, temp_before, heat)
        for tile in range(NY // 8):
            cut = slice(OY + 8 * tile, OY + 8 * tile + 8)
            back = (NZ - 2 * D + D * gz - PITCH * (tile + 1) + NZ) % NZ
            put = pl.ds(8 * tile, 8)
            temp_out[x - D, put] = jnp.where(
                near, pltpu.roll(strip_t[x - D], back, 1), temp[cut]
            )
            speed[x - D, put] = jnp.where(
                near, pltpu.roll(strip_s[x - D], back, 1), fast[cut]
            )

    substep(history.at[5], None, bricks.at[1], 6, main, brick_end)

    speed_copies = []

    def tell(dx, dy, z, number, recv_sem):
        if dy == 0:
            deep_x = 2
            src_y, dst_y, count_y = 14 * z, 8 - 2 * z, 18
        else:
            deep_x = 1
            count_y = 2 if dx == 0 else 1
            src_y = NY - count_y if dy == 1 else 0
            dst_y = 8 - count_y if dy == 1 else 8 + GR
        src_x = {-1: (0, deep_x), 0: (0, NX), 1: (NX - deep_x, deep_x)}[dx]
        dst_x = {-1: 2 + NX, 0: 2, 1: 2 - deep_x}[dx]
        speed_copies.append(send(
            speed.at[pl.ds(*src_x), pl.ds(src_y, count_y)],
            gspeed.at[gz, pl.ds(dst_x, src_x[1]), pl.ds(dst_y, count_y)],
            speed_send.at[number], recv_sem, at(dx, dy, z),
        ))

    for dx in (-1, 1):
        for z in range(2):
            tell(dx, 0, z, len(speed_copies), speed_recv_a.at[dx + 1, gz])
    for dy, z in ((1, 0), (-1, 1)):
        for dx in (-1, 0, 1):
            tell(dx, dy, z, len(speed_copies), speed_recv_b.at[dx + 1, gz])
    tell(0, 0, other, len(speed_copies), speed_recv_a.at[1, gz])
    keep = pltpu.make_async_copy(
        speed.at[:, pl.ds(14 * gz, 18)],
        gspeed.at[gz, pl.ds(2, NX), pl.ds(8 - 2 * gz, 18)],
        local_sem,
    )
    keep.start()

    for copy in lab_copies:
        copy.wait()
    row_g = rows((GY, NZ))
    outside_g = ((row_g < 8) & (gy + gz == 0)) | (
        (row_g >= 8 + GR) & (gy + gz == ngy)
    )

    def border(x, _):
        outside = outside_g | ((x < 2) & (gx == 0)) | ((x >= 2 + NX) & (gx == ngx - 1))
        for half in range(2):
            lab[0, half, x] = jnp.where(outside, 0, lab[0, half, x])
            lab[1, half, x] = jnp.where(outside, -1, lab[1, half, x])
        return 0

    lax.fori_loop(0, GX, border, 0)

    def first_labels(x, _):
        codes = [lab[1, half, x] for half in range(2)]
        sides = pick(lab.at[0], x, codes)
        for half in range(2):
            lab1[half, x] = jnp.where(codes[half] > 0, sides[half], lab[0, half, x])
            reach1[half, x] = lookup(tables, sides[half], codes[half])
        return 0

    lax.fori_loop(1, GX - 1, first_labels, 0)

    def second_labels(x, _):
        codes = [lab[2, half, x] for half in range(2)]
        sides = pick(lab1, x, codes)
        for half in range(2):
            label = jnp.where(codes[half] > 0, sides[half], lab1[half, x])
            grain_out[x - 2, :, pl.ds(half * NZ, NZ)] = label[8 : 8 + GR] >> 6
            reach2[half, x] = lookup(tables, sides[half], codes[half])
        return 0

    lax.fori_loop(2, GX - 2, second_labels, 0)

    for copy in speed_copies:
        copy.wait_send()
    keep.wait()

    def heard(count_x, count_y, recv_sem):
        pltpu.make_async_remote_copy(
            src_ref=speed.at[pl.ds(0, count_x), pl.ds(0, count_y)],
            dst_ref=gspeed.at[0, pl.ds(0, count_x), pl.ds(0, count_y)],
            send_sem=speed_send.at[0], recv_sem=recv_sem,
            device_id=at(0, 0, other), device_id_type=MESH,
        ).wait_recv()

    for z in range(2):
        for dx in (-1, 1):
            heard(2, 18, speed_recv_a.at[dx + 1, z])
            heard(1, 1, speed_recv_b.at[dx + 1, z])
        heard(NX, 2, speed_recv_b.at[1, z])
    heard(NX, 18, speed_recv_a.at[1, other])

    def seeded(x, _):
        for half in range(2):
            grown[half, x] = jnp.where(lab[0, half, x] > 0, gspeed[half, x], 0.0)
        return 0

    lax.fori_loop(0, GX, seeded, 0)

    def first_growth(x, _):
        codes = [lab[1, half, x] for half in range(2)]
        sides = pick(grown, x, codes)
        for half in range(2):
            code = codes[half]
            caught = jnp.maximum(sides[half] - reach1[half, x], 0.0)
            envelope = jnp.where(
                code > 0, caught, jnp.where(code == 0, grown[half, x], 0.0)
            )
            env1[half, x] = envelope
            grown1[half, x] = envelope + jnp.where(lab1[half, x] > 0, gspeed[half, x], 0.0)
        return 0

    lax.fori_loop(1, GX - 1, first_growth, 0)

    def second_growth(x, _):
        codes = [lab[2, half, x] for half in range(2)]
        sides = pick(grown1, x, codes)
        for half in range(2):
            code = codes[half]
            caught = jnp.maximum(sides[half] - reach2[half, x], 0.0)
            envelope = jnp.where(
                code > 0, caught, jnp.where(code == 0, grown1[half, x], env1[half, x])
            )
            env_out[x - 2, :, pl.ds(half * NZ, NZ)] = envelope[8 : 8 + GR]
        return 0

    lax.fori_loop(2, GX - 2, second_growth, 0)


def body(*args):
    vmem = pl.BlockSpec(memory_space=pltpu.VMEM)
    smem = pl.BlockSpec(memory_space=pltpu.SMEM)
    f32, i32 = jnp.float32, jnp.int32
    dma = pltpu.SemaphoreType.DMA
    growth = (2, GX, GY, NZ)
    return pl.pallas_call(
        kernel,
        out_shape=(
            jax.ShapeDtypeStruct((NX, NY, NZ), f32),
            jax.ShapeDtypeStruct((NX, GR, 2 * NZ), f32),
            jax.ShapeDtypeStruct((NX, GR, 2 * NZ), i32),
        ),
        in_specs=[vmem] * 7 + [smem, vmem],
        out_specs=(vmem, vmem, vmem),
        scratch_shapes=[
            pltpu.VMEM((2, EX, EY, NZ), f32),
            pltpu.VMEM((6, EX, EY, NZ), f32),
            pltpu.VMEM((6, EX, 8, NZ), f32),
            pltpu.VMEM((EX, 8, NZ), f32),
            pltpu.VMEM((EX, 8, NZ), f32),
            pltpu.VMEM((EX, 8, NZ), f32),
            pltpu.VMEM((NX, NY, NZ), f32),
            pltpu.VMEM((NX, 8, NZ), f32),
            pltpu.VMEM((NX, 8, NZ), f32),
            pltpu.VMEM((3,) + growth, i32),
            pltpu.VMEM(growth, i32),
            pltpu.VMEM(growth, f32),
            pltpu.VMEM(growth, f32),
            pltpu.VMEM(growth, f32),
            pltpu.VMEM(growth, f32),
            pltpu.VMEM(growth, f32),
            pltpu.VMEM(growth, f32),
            dma((8,)), dma((8,)), dma, dma,
            dma((11,)), dma((3, 2)), dma((3, 2)), dma, dma((8,)), dma((8,)),
        ],
        compiler_params=pltpu.CompilerParams(
            collective_id=0, has_side_effects=True, vmem_limit_bytes=50 << 20
        ),
    )(*args)


def solution(mesh):
    thermal = P("gx", "gy", "gz")
    growth = P("gx", ("gy", "gz"), None)
    placed = (
        thermal, thermal, thermal, growth, growth, growth,
        P(None, "gx", ("gy", "gz"), None), growth, P(),
    )
    return jax.shard_map(
        body, mesh=mesh, in_specs=placed, out_specs=(thermal, growth, growth), check_vma=False
    )
```

time: 345 us -> 70.5 us (0.20)
  the two profiles are of different devices: /device:TPU:128 before, /device:TPU:1 now
where the time goes in v1:
time: 70.5 us; the launch traced here: 70.1 us
  Pallas kernels  59.3 us (84%)
  local copies, waits for them, and re-layouts  10.2 us (14%)
    pallas_call x1, Pallas kernels, body(): pl.pallas_call(kernel, out_shape=(jax.ShapeDtypeStruct((NX, NY, NZ), f32)...  59.3 us
    unnamed x21, local copies, waits for them, and re-layouts  10.2 us

profile of v1, /device:TPU:1, one launch (start us, length us, event | category | flops | bytes accessed | tf_op | source)
XLA Modules:
  0.0 70.1 jit_solution(5139892067831129913)
XLA Ops:
  0.6 0.0 copy-start
  0.6 1.0 %copy-done = s32[2,16,16,256]{3,2,1,0:T(8,128)S(1)} copy-done((s32[2,16,16,256]{3,2,1,0:T(8,128)S(1)}, s32[2,16,16,256]{3,2,1,0:T(8,128)}, u32[]{:S(2)}) %copy-start) | copy-done | bytes 524312
  1.7 0.0 copy-start.1
  1.7 0.9 %copy-done.1 = f32[16,32,128]{2,1,0:T(8,128)S(1)} copy-done((f32[16,32,128]{2,1,0:T(8,128)S(1)}, f32[16,32,128]{2,1,0:T(8,128)}, u32[]{:S(2)}) %copy-start.1) | copy-done | bytes 262168
  2.6 0.0 copy-start.2
  2.6 0.9 %copy-done.2 = f32[16,32,128]{2,1,0:T(8,128)S(1)} copy-done((f32[16,32,128]{2,1,0:T(8,128)S(1)}, f32[16,32,128]{2,1,0:T(8,128)}, u32[]{:S(2)}) %copy-start.2) | copy-done | bytes 262168
  3.6 0.0 copy-start.3
  3.6 0.9 %copy-done.3 = s32[16,32,128]{2,1,0:T(8,128)S(1)} copy-done((s32[16,32,128]{2,1,0:T(8,128)S(1)}, s32[16,32,128]{2,1,0:T(8,128)}, u32[]{:S(2)}) %copy-start.3) | copy-done | bytes 262168
  4.5 0.0 copy-start.4
  4.5 0.9 %copy-done.4 = s32[16,16,256]{2,1,0:T(8,128)S(1)} copy-done((s32[16,16,256]{2,1,0:T(8,128)S(1)}, s32[16,16,256]{2,1,0:T(8,128)}, u32[]{:S(2)}) %copy-start.4) | copy-done | bytes 262168
  5.5 0.0 copy-start.5
  5.5 0.9 %copy-done.5 = s32[16,16,256]{2,1,0:T(8,128)S(1)} copy-done((s32[16,16,256]{2,1,0:T(8,128)S(1)}, s32[16,16,256]{2,1,0:T(8,128)}, u32[]{:S(2)}) %copy-start.5) | copy-done | bytes 262168
  6.4 0.0 copy-start.6
  6.4 0.9 %copy-done.6 = s32[16,16,256]{2,1,0:T(8,128)S(1)} copy-done((s32[16,16,256]{2,1,0:T(8,128)S(1)}, s32[16,16,256]{2,1,0:T(8,128)}, u32[]{:S(2)}) %copy-start.6) | copy-done | bytes 262168
  7.4 0.0 copy-start.7
  7.4 0.7 copy-done.7
  8.1 0.0 copy-start.8
  8.1 0.7 copy-done.8
  8.7 59.3 %shard_map.112 = (f32[16,32,128]{2,1,0:T(8,128)S(1)}, f32[16,16,256]{2,1,0:T(8,128)S(1)}, s32[16,16,256]{2,1,0:T(8,128)S(1)}) custom-call(f32[16,32,128]{2,1,0:T(8,128)S(1)} %copy-done.1, f32[16,32,128]{2,1,0:T(8,128)S(1)} %copy-done.2, s32[16,32,128]{2,1,0:T(8,128)S(1)} %copy-done.3, s32[16,16,256]{2,1,0:T(8,128)S(1)} %copy-done.4, ...), custom_call_target="tpu_custom_call" | custom-call | tf_op jit(solution)/shard_map/pallas_call | solution.py:495
  68.0 0.7 %copy.15 = f32[16,32,128]{2,1,0:T(8,128)} copy(f32[16,32,128]{2,1,0:T(8,128)S(1)} %get-tuple-element.6) | data formatting | bytes 524288
  68.7 0.7 %copy.16 = f32[16,16,256]{2,1,0:T(8,128)} copy(f32[16,16,256]{2,1,0:T(8,128)S(1)} %get-tuple-element.7) | data formatting | bytes 524288
  69.4 0.7 %copy.17 = s32[16,16,256]{2,1,0:T(8,128)} copy(s32[16,16,256]{2,1,0:T(8,128)S(1)} %get-tuple-element.8) | data formatting | bytes 524288
Async XLA Ops:
  0.6 1.0 %copy-start = (s32[2,16,16,256]{3,2,1,0:T(8,128)S(1)}, s32[2,16,16,256]{3,2,1,0:T(8,128)}, u32[]{:S(2)}) copy-start(s32[2,16,16,256]{3,2,1,0:T(8,128)} %captured.1) | copy-start | bytes 1572868
  1.7 0.9 %copy-start.1 = (f32[16,32,128]{2,1,0:T(8,128)S(1)}, f32[16,32,128]{2,1,0:T(8,128)}, u32[]{:S(2)}) copy-start(f32[16,32,128]{2,1,0:T(8,128)} %kelvin.1) | copy-start | bytes 786436
  2.6 0.9 %copy-start.2 = (f32[16,32,128]{2,1,0:T(8,128)S(1)}, f32[16,32,128]{2,1,0:T(8,128)}, u32[]{:S(2)}) copy-start(f32[16,32,128]{2,1,0:T(8,128)} %conductance.1) | copy-start | bytes 786436
  3.6 0.9 %copy-start.3 = (s32[16,32,128]{2,1,0:T(8,128)S(1)}, s32[16,32,128]{2,1,0:T(8,128)}, u32[]{:S(2)}) copy-start(s32[16,32,128]{2,1,0:T(8,128)} %melted.1) | copy-start | bytes 786436
  4.5 0.9 %copy-start.4 = (s32[16,16,256]{2,1,0:T(8,128)S(1)}, s32[16,16,256]{2,1,0:T(8,128)}, u32[]{:S(2)}) copy-start(s32[16,16,256]{2,1,0:T(8,128)} %germ.1) | copy-start | bytes 786436
  5.5 0.9 %copy-start.5 = (s32[16,16,256]{2,1,0:T(8,128)S(1)}, s32[16,16,256]{2,1,0:T(8,128)}, u32[]{:S(2)}) copy-start(s32[16,16,256]{2,1,0:T(8,128)} %nucleus.1) | copy-start | bytes 786436
  6.4 0.9 %copy-start.6 = (s32[16,16,256]{2,1,0:T(8,128)S(1)}, s32[16,16,256]{2,1,0:T(8,128)}, u32[]{:S(2)}) copy-start(s32[16,16,256]{2,1,0:T(8,128)} %pose.1) | copy-start | bytes 786436
  7.4 0.7 copy-start.7
  8.1 0.7 copy-start.8

commit v2 on v1

--- a/solution.py
+++ b/solution.py
@@ -46,39 +46,13 @@
     return pltpu.roll(value, amount % value.shape[axis], axis)
 
 
-class Main:
-    def __init__(self):
-        self.lane_end = lanes((EY, NZ)) == NZ - 1
-
-    def up(self, v):
-        return roll(v, -1, 0)
-
-    def down(self, v):
-        return roll(v, 1, 0)
-
-    def edge(self, flux):
-        return jnp.where(self.lane_end, 0.0, flux)
-
-
-class Strip:
-    def __init__(self):
-        self.first = rows((8, NZ)) == 0
-        self.last = rows((8, NZ)) == 7
-
-    def up(self, v):
-        turned = roll(v, -1, 0)
-        return jnp.where(self.last, roll(turned, -PITCH, 1), turned)
-
-    def down(self, v):
-        turned = roll(v, 1, 0)
-        return jnp.where(self.first, roll(turned, PITCH, 1), turned)
-
-    def edge(self, flux):
-        return flux
-
-
-def substep(src, dst, base, step, form, finish=None):
-    first, stop = step, EX - step
+def shifted(value, amount, axis):
+    return roll(value, amount, value.ndim - 2 + axis)
+
+
+def substep(src, dst, base, step, finish=None):
+    first, count = step, EX - 2 * step
+    lane_end = lanes((EY, NZ)) == NZ - 1
     before_t, before_k = state(src[first - 1], base[first - 1])
     here_t, here_k = state(src[first], base[first])
     into = face(before_t, before_k, here_t, here_k)
@@ -87,9 +61,10 @@
         here_t, here_k, into = carry
         next_t, next_k = state(src[x + 1], base[x + 1])
         out_of = face(here_t, here_k, next_t, next_k)
-        along_y = face(here_t, here_k, form.up(here_t), form.up(here_k))
-        along_z = form.edge(face(here_t, here_k, roll(here_t, -1, 1), roll(here_k, -1, 1)))
-        total = (out_of - into) + (along_y - form.down(along_y)) + (along_z - roll(along_z, 1, 1))
+        along_y = face(here_t, here_k, roll(here_t, -1, 0), roll(here_k, -1, 0))
+        along_z = face(here_t, here_k, roll(here_t, -1, 1), roll(here_k, -1, 1))
+        along_z = jnp.where(lane_end, 0.0, along_z)
+        total = (out_of - into) + (along_y - roll(along_y, 1, 0)) + (along_z - roll(along_z, 1, 1))
         heat = src[x] + 0.2 * total
         if finish is None:
             dst[x] = heat
@@ -97,19 +72,42 @@
             finish(x, here_t, heat)
         return next_t, next_k, out_of
 
-    def pair(i, carry):
-        x = first + 2 * i
-        return slab(x + 1, slab(x, carry))
-
-    lax.fori_loop(0, (stop - first) // 2, pair, (here_t, here_k, into))
-
-
-def outcome(history, x, temp_before, heat):
+    chunk = count // 2
+
+    def several(i, carry):
+        for j in range(chunk):
+            carry = slab(first + chunk * i + j, carry)
+        return carry
+
+    lax.fori_loop(0, 2, several, (here_t, here_k, into))
+
+
+def strip_substep(heat, base, step):
+    temp, cond = state(heat, base)
+    across = face(temp[:-1], cond[:-1], temp[1:], cond[1:])
+    temp, cond = temp[1:-1], cond[1:-1]
+    row = lax.broadcasted_iota(jnp.int32, temp.shape, 1)
+
+    def up(v):
+        turned = roll(v, -1, 1)
+        return jnp.where(row == 7, roll(turned, -PITCH, 2), turned)
+
+    def down(v):
+        turned = roll(v, 1, 1)
+        return jnp.where(row == 0, roll(turned, PITCH, 2), turned)
+
+    along_y = face(temp, cond, up(temp), up(cond))
+    along_z = face(temp, cond, roll(temp, -1, 2), roll(cond, -1, 2))
+    total = (across[1:] - across[:-1]) + (along_y - down(along_y)) + (along_z - roll(along_z, 1, 2))
+    return heat[1:-1] + 0.2 * total, temp
+
+
+def outcome(earlier, temp_before, heat):
     solid = clip03(heat)
     temp = heat - solid * (2.0 / 3.0)
     liquid = solid
-    for s in range(1, 6):
-        liquid = liquid + clip03(history[s, x])
+    for past in earlier:
+        liquid = liquid + clip03(past)
     cooling = (temp_before - temp) * 10.0
     under = jnp.maximum(cooling, 0.0) * (0.5 + liquid * (0.1 / 3.0))
     return temp, under * under
@@ -125,17 +123,17 @@
     return down, up
 
 
-def pick(ref, x, codes):
-    here = (ref[0, x], ref[1, x])
+def pick(ref, x, first, count, codes):
+    here = (ref[0, x, pl.ds(first, count)], ref[1, x, pl.ds(first, count)])
     down, up = shift_z(*here)
     picked = []
     for half in range(2):
         code = codes[half]
         views = (
-            ref[half, x - 1],
-            ref[half, x + 1],
-            roll(here[half], 1, 0),
-            roll(here[half], -1, 0),
+            ref[half, x - 1, pl.ds(first, count)],
+            ref[half, x + 1, pl.ds(first, count)],
+            ref[half, x, pl.ds(first - 1, count)],
+            ref[half, x, pl.ds(first + 1, count)],
             down[half],
             up[half],
         )
@@ -144,6 +142,17 @@
             value = jnp.where(code == number + 1, view, value)
         picked.append(value)
     return picked
+
+
+def loop(start, stop, unroll, step):
+    assert (stop - start) % unroll == 0
+
+    def several(i, _):
+        for j in range(unroll):
+            step(start + unroll * i + j)
+        return 0
+
+    lax.fori_loop(0, (stop - start) // unroll, several, 0)
 
 
 def reach_rows(turns):
@@ -178,8 +187,11 @@
 
 
 def kernel(
-    kelvin, conductance, melted, germ, nucleus, pose, captured, roster, turns,
+    kelvin_hbm, conductance_hbm, melted_hbm, germ_hbm, nucleus_hbm, pose_hbm, captured_hbm,
+    roster_hbm, turns_hbm,
     temp_out, env_out, grain_out,
+    kelvin, conductance, melted, germ, nucleus, pose, captured, roster, turns, load_sem,
+    temp_own, env_own, grain_own, save_sem,
     bricks, history, strip_h, strip_b, strip_out, strip_in, speed,
     strip_t, strip_s, lab, lab1, reach1, reach2, gspeed, grown, grown1, env1,
     heat_send, heat_recv, strip_send, strip_recv,
@@ -201,6 +213,17 @@
     for device in greeted:
         pl.semaphore_signal(barrier, inc=1, device_id=device, device_id_type=MESH)
 
+    loads = [
+        pltpu.make_async_copy(src, dst, load_sem.at[i])
+        for i, (src, dst) in enumerate((
+            (kelvin_hbm, kelvin), (melted_hbm, melted), (conductance_hbm, conductance),
+            (germ_hbm, germ), (nucleus_hbm, nucleus), (pose_hbm, pose),
+            (captured_hbm, captured), (roster_hbm, roster), (turns_hbm, turns),
+        ))
+    ]
+    for load in loads:
+        load.start()
+
     def send(src, dst, send_sem, recv_sem, device):
         copy = pltpu.make_async_remote_copy(
             src_ref=src, dst_ref=dst, send_sem=send_sem, recv_sem=recv_sem,
@@ -211,18 +234,21 @@
 
     own_rows = pl.ds(OY, NY)
 
-    def opening(x, _):
+    def opening(x):
         melt = melted[x].astype(jnp.float32)
         start = kelvin[x] + 1.5 * melt
         bricks[0, D + x, own_rows] = start + 2.0 * jnp.clip(start, 0.0, 1.0)
         bricks[1, D + x, own_rows] = conductance[x] * (0.25 + 0.75 * melt)
-        return 0
-
-    lax.fori_loop(0, NX, opening, 0)
-
+
+    for load in loads[:3]:
+        load.wait()
+    loop(0, NX, 4, opening)
+
+    for load in loads[3:]:
+        load.wait()
     tiles = [roster[0, 0, i] for i in range(8)]
 
-    def seeds(x, _):
+    def seeds(x):
         tile = x // 2
         active = tiles[0] == tile
         for number in tiles[1:]:
@@ -235,9 +261,8 @@
                 lab[1 + g, half, 2 + x, pl.ds(8, GR)] = jnp.where(
                     active, captured[g, x, :, cut], -1
                 )
-        return 0
-
-    lax.fori_loop(0, NX, seeds, 0)
+
+    loop(0, NX, 2, seeds)
 
     pl.semaphore_wait(barrier, len(greeted))
 
@@ -293,7 +318,7 @@
     halo_slot = jnp.logical_not(own_slot) & in_use
     turn = D * (1 - 2 * gz)
 
-    def pack(x, _):
+    def pack(x):
         outside_x = ((x < D) & (gx == 0)) | ((x >= D + NX) & (gx == ngx - 1))
         base = jnp.where(outside_x | outside_y, 0.0, bricks[1, x])
         bricks[1, x] = base
@@ -309,56 +334,52 @@
                 mine = own_slot & (lane8 >= tile * PITCH) & (lane8 < (tile + 1) * PITCH)
                 strip = jnp.where(mine, moved, strip)
             packed.append(strip)
-        strip_h[0, x] = packed[0]
+        strip_h[x] = packed[0]
         strip_b[x] = packed[1]
         strip_out[x] = jnp.where(halo_slot, pltpu.roll(packed[1], (turn + NZ) % NZ, 1), packed[0])
-        return 0
-
-    lax.fori_loop(0, EX, pack, 0)
+
+    loop(0, EX, 4, pack)
     strip_copy = send(
         strip_out, strip_in, strip_send, strip_recv, at(0, 0, other)
     )
 
-    main = Main()
     for step in range(1, 6):
-        substep(
-            history.at[step - 1], history.at[step], bricks.at[1], step, main
-        )
+        substep(history.at[step - 1], history.at[step], bricks.at[1], step)
 
     strip_copy.wait()
 
-    def unpack(x, _):
+    def unpack(x):
         got = strip_in[x]
-        strip_h[0, x] = jnp.where(halo_slot, pltpu.roll(got, (turn + NZ) % NZ, 1), strip_h[0, x])
+        strip_h[x] = jnp.where(halo_slot, pltpu.roll(got, (turn + NZ) % NZ, 1), strip_h[x])
         strip_b[x] = jnp.where(halo_slot, pltpu.roll(got, (2 * turn + NZ) % NZ, 1), strip_b[x])
-        return 0
-
-    lax.fori_loop(0, EX, unpack, 0)
-    form = Strip()
-    for step in range(1, 6):
-        substep(strip_h.at[step - 1], strip_h.at[step], strip_b, step, form)
-
-    def strip_end(x, temp_before, heat):
-        strip_t[x - D], strip_s[x - D] = outcome(strip_h, x, temp_before, heat)
-
-    substep(strip_h.at[5], None, strip_b, 6, form, strip_end)
+
+    loop(0, EX, 14, unpack)
+    heat = strip_h[...]
+    earlier = []
+    for step in range(1, 7):
+        heat, temp_before = strip_substep(heat, strip_b[pl.ds(step - 1, EX + 2 - 2 * step)], step)
+        if step < 6:
+            earlier.append(heat[D - step : D - step + NX])
+    strip_t[...], strip_s[...] = outcome(earlier, temp_before, heat)
 
     near = jnp.where(gz == 0, lane8 - (NZ - D), D - 1 - lane8) >= 0
 
     def brick_end(x, temp_before, heat):
-        temp, fast = outcome(history, x, temp_before, heat)
+        temp, fast = outcome([history[s, x] for s in range(1, 6)], temp_before, heat)
         for tile in range(NY // 8):
             cut = slice(OY + 8 * tile, OY + 8 * tile + 8)
             back = (NZ - 2 * D + D * gz - PITCH * (tile + 1) + NZ) % NZ
             put = pl.ds(8 * tile, 8)
-            temp_out[x - D, put] = jnp.where(
+            temp_own[x - D, put] = jnp.where(
                 near, pltpu.roll(strip_t[x - D], back, 1), temp[cut]
             )
             speed[x - D, put] = jnp.where(
                 near, pltpu.roll(strip_s[x - D], back, 1), fast[cut]
             )
 
-    substep(history.at[5], None, bricks.at[1], 6, main, brick_end)
+    substep(history.at[5], None, bricks.at[1], 6, brick_end)
+    temp_save = pltpu.make_async_copy(temp_own, temp_out, save_sem.at[0])
+    temp_save.start()
 
     speed_copies = []
 
@@ -400,35 +421,36 @@
         (row_g >= 8 + GR) & (gy + gz == ngy)
     )
 
-    def border(x, _):
+    def border(x):
         outside = outside_g | ((x < 2) & (gx == 0)) | ((x >= 2 + NX) & (gx == ngx - 1))
         for half in range(2):
             lab[0, half, x] = jnp.where(outside, 0, lab[0, half, x])
             lab[1, half, x] = jnp.where(outside, -1, lab[1, half, x])
-        return 0
-
-    lax.fori_loop(0, GX, border, 0)
-
-    def first_labels(x, _):
-        codes = [lab[1, half, x] for half in range(2)]
-        sides = pick(lab.at[0], x, codes)
-        for half in range(2):
-            lab1[half, x] = jnp.where(codes[half] > 0, sides[half], lab[0, half, x])
-            reach1[half, x] = lookup(tables, sides[half], codes[half])
-        return 0
-
-    lax.fori_loop(1, GX - 1, first_labels, 0)
-
-    def second_labels(x, _):
-        codes = [lab[2, half, x] for half in range(2)]
-        sides = pick(lab1, x, codes)
-        for half in range(2):
-            label = jnp.where(codes[half] > 0, sides[half], lab1[half, x])
-            grain_out[x - 2, :, pl.ds(half * NZ, NZ)] = label[8 : 8 + GR] >> 6
-            reach2[half, x] = lookup(tables, sides[half], codes[half])
-        return 0
-
-    lax.fori_loop(2, GX - 2, second_labels, 0)
+
+    loop(0, GX, 2, border)
+    wide = pl.ds(7, 24)
+    own = pl.ds(8, GR)
+
+    def first_labels(x):
+        codes = [lab[1, half, x, wide] for half in range(2)]
+        sides = pick(lab.at[0], x, 7, 24, codes)
+        for half in range(2):
+            lab1[half, x, wide] = jnp.where(codes[half] > 0, sides[half], lab[0, half, x, wide])
+            reach1[half, x, wide] = lookup(tables, sides[half], codes[half])
+
+    loop(1, GX - 1, 3, first_labels)
+
+    def second_labels(x):
+        codes = [lab[2, half, x, own] for half in range(2)]
+        sides = pick(lab1, x, 8, GR, codes)
+        for half in range(2):
+            label = jnp.where(codes[half] > 0, sides[half], lab1[half, x, own])
+            grain_own[x - 2, :, pl.ds(half * NZ, NZ)] = label >> 6
+            reach2[half, x, own] = lookup(tables, sides[half], codes[half])
+
+    loop(2, GX - 2, 4, second_labels)
+    grain_save = pltpu.make_async_copy(grain_own, grain_out, save_sem.at[1])
+    grain_save.start()
 
     for copy in speed_copies:
         copy.wait_send()
@@ -449,62 +471,90 @@
         heard(NX, 2, speed_recv_b.at[1, z])
     heard(NX, 18, speed_recv_a.at[1, other])
 
-    def seeded(x, _):
+    def seeded(x):
         for half in range(2):
             grown[half, x] = jnp.where(lab[0, half, x] > 0, gspeed[half, x], 0.0)
-        return 0
-
-    lax.fori_loop(0, GX, seeded, 0)
-
-    def first_growth(x, _):
-        codes = [lab[1, half, x] for half in range(2)]
-        sides = pick(grown, x, codes)
+
+    loop(0, GX, 4, seeded)
+
+    def first_growth(x):
+        codes = [lab[1, half, x, wide] for half in range(2)]
+        sides = pick(grown, x, 7, 24, codes)
         for half in range(2):
             code = codes[half]
-            caught = jnp.maximum(sides[half] - reach1[half, x], 0.0)
+            caught = jnp.maximum(sides[half] - reach1[half, x, wide], 0.0)
             envelope = jnp.where(
-                code > 0, caught, jnp.where(code == 0, grown[half, x], 0.0)
+                code > 0, caught, jnp.where(code == 0, grown[half, x, wide], 0.0)
             )
-            env1[half, x] = envelope
-            grown1[half, x] = envelope + jnp.where(lab1[half, x] > 0, gspeed[half, x], 0.0)
-        return 0
-
-    lax.fori_loop(1, GX - 1, first_growth, 0)
-
-    def second_growth(x, _):
-        codes = [lab[2, half, x] for half in range(2)]
-        sides = pick(grown1, x, codes)
+            env1[half, x, wide] = envelope
+            grown1[half, x, wide] = envelope + jnp.where(
+                lab1[half, x, wide] > 0, gspeed[half, x, wide], 0.0
+            )
+
+    loop(1, GX - 1, 3, first_growth)
+
+    def second_growth(x):
+        codes = [lab[2, half, x, own] for half in range(2)]
+        sides = pick(grown1, x, 8, GR, codes)
         for half in range(2):
             code = codes[half]
-            caught = jnp.maximum(sides[half] - reach2[half, x], 0.0)
-            envelope = jnp.where(
-                code > 0, caught, jnp.where(code == 0, grown1[half, x], env1[half, x])
-            )
-            env_out[x - 2, :, pl.ds(half * NZ, NZ)] = envelope[8 : 8 + GR]
-        return 0
-
-    lax.fori_loop(2, GX - 2, second_growth, 0)
+            caught = jnp.maximum(sides[half] - reach2[half, x, own], 0.0)
+            kept = jnp.where(code == 0, grown1[half, x, own], env1[half, x, own])
+            env_own[x - 2, :, pl.ds(half * NZ, NZ)] = jnp.where(code > 0, caught, kept)
+
+    loop(2, GX - 2, 4, second_growth)
+    env_save = pltpu.make_async_copy(env_own, env_out, save_sem.at[2])
+    env_save.start()
+    for save in (temp_save, grain_save, env_save):
+        save.wait()
+
+
+def handing_on(*refs):
+    sources, targets, held, sems = refs[:3], refs[3:6], refs[6:9], refs[9]
+    fetches = [pltpu.make_async_copy(sources[i], held[i], sems.at[0, i]) for i in range(3)]
+    stores = [pltpu.make_async_copy(held[i], targets[i], sems.at[1, i]) for i in range(3)]
+    for fetch in fetches:
+        fetch.start()
+    for fetch, store in zip(fetches, stores):
+        fetch.wait()
+        store.start()
+    for store in stores:
+        store.wait()
 
 
 def body(*args):
-    vmem = pl.BlockSpec(memory_space=pltpu.VMEM)
-    smem = pl.BlockSpec(memory_space=pltpu.SMEM)
+    hbm = pl.BlockSpec(memory_space=pltpu.HBM)
     f32, i32 = jnp.float32, jnp.int32
     dma = pltpu.SemaphoreType.DMA
     growth = (2, GX, GY, NZ)
-    return pl.pallas_call(
+    results = (
+        jax.ShapeDtypeStruct((NX, NY, NZ), f32),
+        jax.ShapeDtypeStruct((NX, GR, 2 * NZ), f32),
+        jax.ShapeDtypeStruct((NX, GR, 2 * NZ), i32),
+    )
+    made = pl.pallas_call(
         kernel,
-        out_shape=(
-            jax.ShapeDtypeStruct((NX, NY, NZ), f32),
-            jax.ShapeDtypeStruct((NX, GR, 2 * NZ), f32),
-            jax.ShapeDtypeStruct((NX, GR, 2 * NZ), i32),
-        ),
-        in_specs=[vmem] * 7 + [smem, vmem],
-        out_specs=(vmem, vmem, vmem),
+        out_shape=results,
+        in_specs=[hbm] * 9,
+        out_specs=(hbm, hbm, hbm),
         scratch_shapes=[
+            pltpu.VMEM((NX, NY, NZ), f32),
+            pltpu.VMEM((NX, NY, NZ), f32),
+            pltpu.VMEM((NX, NY, NZ), i32),
+            pltpu.VMEM((NX, GR, 2 * NZ), i32),
+            pltpu.VMEM((NX, GR, 2 * NZ), i32),
+            pltpu.VMEM((NX, GR, 2 * NZ), i32),
+            pltpu.VMEM((2, NX, GR, 2 * NZ), i32),
+            pltpu.SMEM((1, 1, 8), i32),
+            pltpu.VMEM((3, 64), f32),
+            dma((9,)),
+            pltpu.VMEM((NX, NY, NZ), f32),
+            pltpu.VMEM((NX, GR, 2 * NZ), f32),
+            pltpu.VMEM((NX, GR, 2 * NZ), i32),
+            dma((3,)),
             pltpu.VMEM((2, EX, EY, NZ), f32),
             pltpu.VMEM((6, EX, EY, NZ), f32),
-            pltpu.VMEM((6, EX, 8, NZ), f32),
+            pltpu.VMEM((EX, 8, NZ), f32),
             pltpu.VMEM((EX, 8, NZ), f32),
             pltpu.VMEM((EX, 8, NZ), f32),
             pltpu.VMEM((EX, 8, NZ), f32),
@@ -523,9 +573,17 @@
             dma((11,)), dma((3, 2)), dma((3, 2)), dma, dma((8,)), dma((8,)),
         ],
         compiler_params=pltpu.CompilerParams(
-            collective_id=0, has_side_effects=True, vmem_limit_bytes=50 << 20
+            collective_id=0, has_side_effects=True, vmem_limit_bytes=62 << 20
         ),
     )(*args)
+    return pl.pallas_call(
+        handing_on,
+        out_shape=results,
+        in_specs=[hbm] * 3,
+        out_specs=(hbm, hbm, hbm),
+        scratch_shapes=[pltpu.VMEM(r.shape, r.dtype) for r in results] + [dma((2, 3))],
+        compiler_params=pltpu.CompilerParams(vmem_limit_bytes=62 << 20),
+    )(*made)
 
 
 def solution(mesh):

time: 70.5 us -> 42.4 us (0.60)
  Pallas kernels: 59.3 us -> 41.6 us
  local copies, waits for them, and re-layouts: 10.2 us -> 0 us
    pallas_call x1 -> x2, Pallas kernels: 59.3 us -> 41.6 us  [the longest x1 39.8 us: body(): pl.pallas_call(kernel, out_shape=results, in_specs=[hbm] * 9, out_specs=(...]
    unnamed x21 -> x0, local copies, waits for them, and re-layouts: 10.2 us -> none
where the time goes in v2:
time: 42.4 us; the launch traced here: 42.3 us
  Pallas kernels  41.6 us (98%)
  between operations  0.64 us (2%)
    pallas_call x1, Pallas kernels, body(): pl.pallas_call(kernel, out_shape=results, in_specs=[hbm] * 9, out_specs=(...  39.8 us
    pallas_call x1, Pallas kernels, body(): pl.pallas_call(handing_on, out_shape=results, in_specs=[hbm] * 3, out_spe...  1.88 us

profile of v2, /device:TPU:1, one launch (start us, length us, event | category | flops | bytes accessed | tf_op | source)
XLA Modules:
  0.0 42.3 jit_solution(10523567175039491448)
XLA Ops:
  0.6 39.8 %shard_map.112 = (f32[16,32,128]{2,1,0:T(8,128)}, f32[16,16,256]{2,1,0:T(8,128)}, s32[16,16,256]{2,1,0:T(8,128)}) custom-call(f32[16,32,128]{2,1,0:T(8,128)} %kelvin_hbm.1, f32[16,32,128]{2,1,0:T(8,128)} %conductance_hbm.1, s32[16,32,128]{2,1,0:T(8,128)} %melted_hbm.1, s32[16,16,256]{2,1,0:T(8,128)} %germ_hbm.1, s32[16,16,256]{2,1,0:T(8,128)} %nucleus_hbm.1, ...), custom_call_target="tpu_custom_call" | custom-call | tf_op jit(solution)/shard_map/pallas_call | solution.py:535
  40.4 1.9 %shard_map.113 = (f32[16,32,128]{2,1,0:T(8,128)}, f32[16,16,256]{2,1,0:T(8,128)}, s32[16,16,256]{2,1,0:T(8,128)}) custom-call(f32[16,32,128]{2,1,0:T(8,128)} %get-tuple-element.6.refs_0_, f32[16,16,256]{2,1,0:T(8,128)} %get-tuple-element.7.refs_1_, s32[16,16,256]{2,1,0:T(8,128)} %get-tuple-element.8.refs_2_), custom_call_target="tpu_custom_call" | custom-call | tf_op jit(solution)/shard_map/pallas_call | solution.py:579

commit v3 on v2

--- a/solution.py
+++ b/solution.py
@@ -80,6 +80,25 @@
         return carry
 
     lax.fori_loop(0, 2, several, (here_t, here_k, into))
+
+
+def last_rows(before, history, base, first):
+    near, own = pl.ds(first, 8), pl.ds(D, NX)
+    heat = before[pl.ds(D - 1, NX + 2), near]
+    temp, cond = state(heat, base[pl.ds(D - 1, NX + 2), near])
+    across = face(temp[:-1], cond[:-1], temp[1:], cond[1:])
+    temp, cond = temp[1:-1], cond[1:-1]
+    lane_end = lax.broadcasted_iota(jnp.int32, temp.shape, 2) == NZ - 1
+    along_y = face(temp, cond, roll(temp, -1, 1), roll(cond, -1, 1))
+    along_z = face(temp, cond, roll(temp, -1, 2), roll(cond, -1, 2))
+    along_z = jnp.where(lane_end, 0.0, along_z)
+    total = (
+        (across[1:] - across[:-1])
+        + (along_y - roll(along_y, 1, 1))
+        + (along_z - roll(along_z, 1, 2))
+    )
+    earlier = [history[s, own, near] for s in range(1, 6)]
+    return outcome(earlier, temp, heat[1:-1] + 0.2 * total)[1]
 
 
 def strip_substep(heat, base, step):
@@ -193,7 +212,7 @@
     kelvin, conductance, melted, germ, nucleus, pose, captured, roster, turns, load_sem,
     temp_own, env_own, grain_own, save_sem,
     bricks, history, strip_h, strip_b, strip_out, strip_in, speed,
-    strip_t, strip_s, lab, lab1, reach1, reach2, gspeed, grown, grown1, env1,
+    far, strip_t, strip_s, lab, lab1, reach1, reach2, gspeed, grown, grown1, env1,
     heat_send, heat_recv, strip_send, strip_recv,
     speed_send, speed_recv_a, speed_recv_b, local_sem, lab_send, lab_recv,
 ):
@@ -205,7 +224,7 @@
 
     other = 1 - gz
     cross = 2 * gz - 1
-    xy = [(dx, dy) for dx in (-1, 0, 1) for dy in (-1, 0, 1) if (dx, dy) != (0, 0)]
+    xy = [(0, -1), (0, 1), (-1, -1), (1, 1), (-1, 1), (1, -1), (-1, 0), (1, 0)]
     greeted = [at(dx, dy, gz) for dx, dy in xy]
     greeted += [at(dx, 0, other) for dx in (-1, 0, 1)]
     greeted += [at(dx, cross, other) for dx in (-1, 0, 1)]
@@ -278,6 +297,50 @@
             bricks.at[:, pl.ds(dst_x, src_x[1]), pl.ds(dst_y, src_y[1])],
             heat_send.at[i], heat_recv.at[i], at(dx, dy, gz),
         ))
+
+    row_x, row_y, row_z = reach_rows(turns[...])
+    tables = [
+        jnp.broadcast_to(jnp.concatenate(pair, axis=1), (8, NZ))
+        for pair in ((row_x, row_y), (row_z, row_z))
+    ]
+
+    for copy in copies:
+        copy.wait()
+
+    lane8 = lanes((8, NZ))
+    row_all = rows((EY, NZ))
+    outside_y = ((row_all < OY) & (gy == 0)) | ((row_all >= OY + NY) & (gy == ngy - 1))
+    slot = lane8
+    for tile in range(1, EY // 8):
+        slot = jnp.where(lane8 >= tile * PITCH, lane8 - tile * PITCH, slot)
+    in_use = lane8 < PITCH * (EY // 8)
+    own_slot = (slot >= D * gz) & (slot < D * gz + 2 * D)
+    halo_slot = jnp.logical_not(own_slot) & in_use
+    turn = D * (1 - 2 * gz)
+
+    def pack(x):
+        outside_x = ((x < D) & (gx == 0)) | ((x >= D + NX) & (gx == ngx - 1))
+        base = jnp.where(outside_x | outside_y, 0.0, bricks[1, x])
+        bricks[1, x] = base
+        heat = bricks[0, x]
+        packed = []
+        for value in (heat, base):
+            strip = jnp.zeros((8, NZ), jnp.float32)
+            for tile in range(EY // 8):
+                moved = pltpu.roll(
+                    value[8 * tile : 8 * tile + 8], (PITCH * tile + 2 * D - D * gz) % NZ, 1
+                )
+                mine = own_slot & (lane8 >= tile * PITCH) & (lane8 < (tile + 1) * PITCH)
+                strip = jnp.where(mine, moved, strip)
+            packed.append(strip)
+        strip_h[x] = packed[0]
+        strip_b[x] = packed[1]
+        strip_out[x] = jnp.where(halo_slot, pltpu.roll(packed[1], (turn + NZ) % NZ, 1), packed[0])
+
+    loop(0, EX, 4, pack)
+    strip_copy = send(
+        strip_out, strip_in, strip_send, strip_recv, at(0, 0, other)
+    )
 
     lab_copies = []
     for i, (dx, dg) in enumerate(xy):
@@ -298,53 +361,9 @@
             lab_send.at[i], lab_recv.at[i], device,
         ))
 
-    row_x, row_y, row_z = reach_rows(turns[...])
-    tables = [
-        jnp.broadcast_to(jnp.concatenate(pair, axis=1), (8, NZ))
-        for pair in ((row_x, row_y), (row_z, row_z))
-    ]
-
-    for copy in copies:
-        copy.wait()
-
-    lane8 = lanes((8, NZ))
-    row_all = rows((EY, NZ))
-    outside_y = ((row_all < OY) & (gy == 0)) | ((row_all >= OY + NY) & (gy == ngy - 1))
-    slot = lane8
-    for tile in range(1, EY // 8):
-        slot = jnp.where(lane8 >= tile * PITCH, lane8 - tile * PITCH, slot)
-    in_use = lane8 < PITCH * (EY // 8)
-    own_slot = (slot >= D * gz) & (slot < D * gz + 2 * D)
-    halo_slot = jnp.logical_not(own_slot) & in_use
-    turn = D * (1 - 2 * gz)
-
-    def pack(x):
-        outside_x = ((x < D) & (gx == 0)) | ((x >= D + NX) & (gx == ngx - 1))
-        base = jnp.where(outside_x | outside_y, 0.0, bricks[1, x])
-        bricks[1, x] = base
-        heat = bricks[0, x]
-        history[0, x] = heat
-        packed = []
-        for value in (heat, base):
-            strip = jnp.zeros((8, NZ), jnp.float32)
-            for tile in range(EY // 8):
-                moved = pltpu.roll(
-                    value[8 * tile : 8 * tile + 8], (PITCH * tile + 2 * D - D * gz) % NZ, 1
-                )
-                mine = own_slot & (lane8 >= tile * PITCH) & (lane8 < (tile + 1) * PITCH)
-                strip = jnp.where(mine, moved, strip)
-            packed.append(strip)
-        strip_h[x] = packed[0]
-        strip_b[x] = packed[1]
-        strip_out[x] = jnp.where(halo_slot, pltpu.roll(packed[1], (turn + NZ) % NZ, 1), packed[0])
-
-    loop(0, EX, 4, pack)
-    strip_copy = send(
-        strip_out, strip_in, strip_send, strip_recv, at(0, 0, other)
-    )
-
     for step in range(1, 6):
-        substep(history.at[step - 1], history.at[step], bricks.at[1], step)
+        before = bricks.at[0] if step == 1 else history.at[step - 1]
+        substep(before, history.at[step], bricks.at[1], step)
 
     strip_copy.wait()
 
@@ -363,6 +382,41 @@
     strip_t[...], strip_s[...] = outcome(earlier, temp_before, heat)
 
     near = jnp.where(gz == 0, lane8 - (NZ - D), D - 1 - lane8) >= 0
+
+    speed_copies = []
+
+    def tell(dx, dy, z, number, recv_sem):
+        if dy == 0:
+            deep_x = 2
+            src_y, dst_y, count_y = 14 * z, 8 - 2 * z, 18
+        else:
+            deep_x = 1
+            count_y = 2 if dx == 0 else 1
+            src_y = 2 - count_y if dy == 1 else 0
+            dst_y = 8 - count_y if dy == 1 else 8 + GR
+        src_x = {-1: (0, deep_x), 0: (0, NX), 1: (NX - deep_x, deep_x)}[dx]
+        dst_x = {-1: 2 + NX, 0: 2, 1: 2 - deep_x}[dx]
+        source = speed if dy == 0 else far.at[(1 - dy) // 2]
+        speed_copies.append(send(
+            source.at[pl.ds(*src_x), pl.ds(src_y, count_y)],
+            gspeed.at[gz, pl.ds(dst_x, src_x[1]), pl.ds(dst_y, count_y)],
+            speed_send.at[number], recv_sem, at(dx, dy, z),
+        ))
+
+    turned = [
+        pltpu.roll(strip_s[...], (NZ - 2 * D + D * gz - PITCH * (tile + 1) + NZ) % NZ, 2)
+        for tile in (NY // 8 - 1, 0)
+    ]
+    near_all = jnp.broadcast_to(near[None], (NX, 8, NZ))
+    upper = last_rows(history.at[5], history, bricks.at[1], OY + NY - 7)
+    upper = jnp.where(near_all, turned[0], roll(upper, 1, 1))
+    lower = last_rows(history.at[5], history, bricks.at[1], OY - 1)
+    lower = jnp.where(near_all, turned[1], roll(lower, -1, 1))
+    far[0, :, pl.ds(0, 2)] = upper[:, 6:8]
+    far[1, :, pl.ds(0, 2)] = lower[:, 0:2]
+    for dx in (0, -1, 1):
+        for dy, z in ((1, 0), (-1, 1)):
+            tell(dx, dy, z, len(speed_copies), speed_recv_b.at[dx + 1, gz])
 
     def brick_end(x, temp_before, heat):
         temp, fast = outcome([history[s, x] for s in range(1, 6)], temp_before, heat)
@@ -381,31 +435,9 @@
     temp_save = pltpu.make_async_copy(temp_own, temp_out, save_sem.at[0])
     temp_save.start()
 
-    speed_copies = []
-
-    def tell(dx, dy, z, number, recv_sem):
-        if dy == 0:
-            deep_x = 2
-            src_y, dst_y, count_y = 14 * z, 8 - 2 * z, 18
-        else:
-            deep_x = 1
-            count_y = 2 if dx == 0 else 1
-            src_y = NY - count_y if dy == 1 else 0
-            dst_y = 8 - count_y if dy == 1 else 8 + GR
-        src_x = {-1: (0, deep_x), 0: (0, NX), 1: (NX - deep_x, deep_x)}[dx]
-        dst_x = {-1: 2 + NX, 0: 2, 1: 2 - deep_x}[dx]
-        speed_copies.append(send(
-            speed.at[pl.ds(*src_x), pl.ds(src_y, count_y)],
-            gspeed.at[gz, pl.ds(dst_x, src_x[1]), pl.ds(dst_y, count_y)],
-            speed_send.at[number], recv_sem, at(dx, dy, z),
-        ))
-
     for dx in (-1, 1):
         for z in range(2):
             tell(dx, 0, z, len(speed_copies), speed_recv_a.at[dx + 1, gz])
-    for dy, z in ((1, 0), (-1, 1)):
-        for dx in (-1, 0, 1):
-            tell(dx, dy, z, len(speed_copies), speed_recv_b.at[dx + 1, gz])
     tell(0, 0, other, len(speed_copies), speed_recv_a.at[1, gz])
     keep = pltpu.make_async_copy(
         speed.at[:, pl.ds(14 * gz, 18)],
@@ -559,6 +591,7 @@
             pltpu.VMEM((EX, 8, NZ), f32),
             pltpu.VMEM((EX, 8, NZ), f32),
             pltpu.VMEM((NX, NY, NZ), f32),
+            pltpu.VMEM((2, NX, 8, NZ), f32),
             pltpu.VMEM((NX, 8, NZ), f32),
             pltpu.VMEM((NX, 8, NZ), f32),
             pltpu.VMEM((3,) + growth, i32),
@@ -570,7 +603,7 @@
             pltpu.VMEM(growth, f32),
             pltpu.VMEM(growth, f32),
             dma((8,)), dma((8,)), dma, dma,
-            dma((11,)), dma((3, 2)), dma((3, 2)), dma, dma((8,)), dma((8,)),
+            dma((14,)), dma((3, 2)), dma((3, 2)), dma, dma((8,)), dma((8,)),
         ],
         compiler_params=pltpu.CompilerParams(
             collective_id=0, has_side_effects=True, vmem_limit_bytes=62 << 20

time: 42.4 us -> 40.4 us (0.953)
  Pallas kernels: 41.6 us -> 39.7 us
    pallas_call x1, Pallas kernels: 39.8 us -> 37.8 us  [body(): pl.pallas_call(kernel, out_shape=results, in_specs=[hbm] * 9, out_specs=(...]
where the time goes in v3:
time: 40.4 us; the launch traced here: 40.3 us
  Pallas kernels  39.7 us (98%)
  between operations  0.64 us (2%)
    pallas_call x1, Pallas kernels, body(): pl.pallas_call(kernel, out_shape=results, in_specs=[hbm] * 9, out_specs=(...  37.8 us
    pallas_call x1, Pallas kernels, body(): pl.pallas_call(handing_on, out_shape=results, in_specs=[hbm] * 3, out_spe...  1.88 us

profile of v3, /device:TPU:1, one launch (start us, length us, event | category | flops | bytes accessed | tf_op | source)
XLA Modules:
  0.0 40.3 jit_solution(7159524004854818290)
XLA Ops:
  0.6 37.8 %shard_map.112 = (f32[16,32,128]{2,1,0:T(8,128)}, f32[16,16,256]{2,1,0:T(8,128)}, s32[16,16,256]{2,1,0:T(8,128)}) custom-call(f32[16,32,128]{2,1,0:T(8,128)} %kelvin_hbm.1, f32[16,32,128]{2,1,0:T(8,128)} %conductance_hbm.1, s32[16,32,128]{2,1,0:T(8,128)} %melted_hbm.1, s32[16,16,256]{2,1,0:T(8,128)} %germ_hbm.1, s32[16,16,256]{2,1,0:T(8,128)} %nucleus_hbm.1, ...), custom_call_target="tpu_custom_call" | custom-call | tf_op jit(solution)/shard_map/pallas_call | solution.py:567
  38.4 1.9 %shard_map.113 = (f32[16,32,128]{2,1,0:T(8,128)}, f32[16,16,256]{2,1,0:T(8,128)}, s32[16,16,256]{2,1,0:T(8,128)}) custom-call(f32[16,32,128]{2,1,0:T(8,128)} %get-tuple-element.6.refs_0_, f32[16,16,256]{2,1,0:T(8,128)} %get-tuple-element.7.refs_1_, s32[16,16,256]{2,1,0:T(8,128)} %get-tuple-element.8.refs_2_), custom_call_target="tpu_custom_call" | custom-call | tf_op jit(solution)/shard_map/pallas_call | solution.py:612

commit v4 on v3

--- a/solution.py
+++ b/solution.py
@@ -156,7 +156,7 @@
             down[half],
             up[half],
         )
-        value = jnp.zeros_like(here[half])
+        value = here[half]
         for number, view in enumerate(views):
             value = jnp.where(code == number + 1, view, value)
         picked.append(value)
@@ -201,7 +201,7 @@
         index = pose[cut] + ((axis[cut] & 1) << 6)
         xy = jnp.take_along_axis(tables[0], index, axis=1, mode="promise_in_bounds")
         z = jnp.take_along_axis(tables[1], index, axis=1, mode="promise_in_bounds")
-        parts.append(jnp.where(axis[cut] == 2, z, xy))
+        parts.append(jnp.where(code[cut] > 0, jnp.where(axis[cut] == 2, z, xy), 0.0))
     return jnp.concatenate(parts, axis=0)
 
 
@@ -212,7 +212,7 @@
     kelvin, conductance, melted, germ, nucleus, pose, captured, roster, turns, load_sem,
     temp_own, env_own, grain_own, save_sem,
     bricks, history, strip_h, strip_b, strip_out, strip_in, speed,
-    far, strip_t, strip_s, lab, lab1, reach1, reach2, gspeed, grown, grown1, env1,
+    far, strip_t, strip_s, lab, lab1, reach1, reach2, gspeed, grown1, env1,
     heat_send, heat_recv, strip_send, strip_recv,
     speed_send, speed_recv_a, speed_recv_b, local_sem, lab_send, lab_recv,
 ):
@@ -304,12 +304,7 @@
         for pair in ((row_x, row_y), (row_z, row_z))
     ]
 
-    for copy in copies:
-        copy.wait()
-
     lane8 = lanes((8, NZ))
-    row_all = rows((EY, NZ))
-    outside_y = ((row_all < OY) & (gy == 0)) | ((row_all >= OY + NY) & (gy == ngy - 1))
     slot = lane8
     for tile in range(1, EY // 8):
         slot = jnp.where(lane8 >= tile * PITCH, lane8 - tile * PITCH, slot)
@@ -318,26 +313,48 @@
     halo_slot = jnp.logical_not(own_slot) & in_use
     turn = D * (1 - 2 * gz)
 
-    def pack(x):
+    def pack(x, ref, values, strip):
+        for tile, value in values:
+            moved = pltpu.roll(value, (PITCH * tile + 2 * D - D * gz) % NZ, 1)
+            mine = own_slot & (lane8 >= tile * PITCH) & (lane8 < (tile + 1) * PITCH)
+            strip = jnp.where(mine, moved, strip)
+        ref[x] = strip
+        return strip
+
+    empty = jnp.zeros((8, NZ), jnp.float32)
+    inside = range(OY // 8, (OY + NY) // 8)
+
+    def pack_own(x):
+        for part, ref in enumerate((strip_h, strip_b)):
+            pack(x, ref, [(tile, bricks[part, x, pl.ds(8 * tile, 8)]) for tile in inside], empty)
+
+    loop(D, D + NX, 4, pack_own)
+
+    for copy in copies:
+        copy.wait()
+
+    def pack_halo(x, tiles, begun):
         outside_x = ((x < D) & (gx == 0)) | ((x >= D + NX) & (gx == ngx - 1))
-        base = jnp.where(outside_x | outside_y, 0.0, bricks[1, x])
-        bricks[1, x] = base
-        heat = bricks[0, x]
-        packed = []
-        for value in (heat, base):
-            strip = jnp.zeros((8, NZ), jnp.float32)
-            for tile in range(EY // 8):
-                moved = pltpu.roll(
-                    value[8 * tile : 8 * tile + 8], (PITCH * tile + 2 * D - D * gz) % NZ, 1
-                )
-                mine = own_slot & (lane8 >= tile * PITCH) & (lane8 < (tile + 1) * PITCH)
-                strip = jnp.where(mine, moved, strip)
-            packed.append(strip)
-        strip_h[x] = packed[0]
-        strip_b[x] = packed[1]
-        strip_out[x] = jnp.where(halo_slot, pltpu.roll(packed[1], (turn + NZ) % NZ, 1), packed[0])
-
-    loop(0, EX, 4, pack)
+        bases = []
+        for tile in tiles:
+            outside = outside_x
+            if tile == 0:
+                outside = outside | (gy == 0)
+            if tile == EY // 8 - 1:
+                outside = outside | (gy == ngy - 1)
+            put = pl.ds(8 * tile, 8)
+            base = jnp.where(outside, 0.0, bricks[1, x, put])
+            bricks[1, x, put] = base
+            bases.append((tile, base))
+        heats = [(tile, bricks[0, x, pl.ds(8 * tile, 8)]) for tile in tiles]
+        heat = pack(x, strip_h, heats, strip_h[x] if begun else empty)
+        base = pack(x, strip_b, bases, strip_b[x] if begun else empty)
+        strip_out[x] = jnp.where(halo_slot, pltpu.roll(base, (turn + NZ) % NZ, 1), heat)
+
+    every = range(EY // 8)
+    loop(0, D, 3, lambda x: pack_halo(x, every, False))
+    loop(D + NX, EX, 3, lambda x: pack_halo(x, every, False))
+    loop(D, D + NX, 4, lambda x: pack_halo(x, (0, EY // 8 - 1), True))
     strip_copy = send(
         strip_out, strip_in, strip_send, strip_recv, at(0, 0, other)
     )
@@ -467,7 +484,7 @@
         codes = [lab[1, half, x, wide] for half in range(2)]
         sides = pick(lab.at[0], x, 7, 24, codes)
         for half in range(2):
-            lab1[half, x, wide] = jnp.where(codes[half] > 0, sides[half], lab[0, half, x, wide])
+            lab1[half, x, wide] = sides[half]
             reach1[half, x, wide] = lookup(tables, sides[half], codes[half])
 
     loop(1, GX - 1, 3, first_labels)
@@ -476,8 +493,7 @@
         codes = [lab[2, half, x, own] for half in range(2)]
         sides = pick(lab1, x, 8, GR, codes)
         for half in range(2):
-            label = jnp.where(codes[half] > 0, sides[half], lab1[half, x, own])
-            grain_own[x - 2, :, pl.ds(half * NZ, NZ)] = label >> 6
+            grain_own[x - 2, :, pl.ds(half * NZ, NZ)] = sides[half] >> 6
             reach2[half, x, own] = lookup(tables, sides[half], codes[half])
 
     loop(2, GX - 2, 4, second_labels)
@@ -503,25 +519,15 @@
         heard(NX, 2, speed_recv_b.at[1, z])
     heard(NX, 18, speed_recv_a.at[1, other])
 
-    def seeded(x):
-        for half in range(2):
-            grown[half, x] = jnp.where(lab[0, half, x] > 0, gspeed[half, x], 0.0)
-
-    loop(0, GX, 4, seeded)
-
     def first_growth(x):
         codes = [lab[1, half, x, wide] for half in range(2)]
-        sides = pick(grown, x, 7, 24, codes)
+        sides = pick(gspeed, x, 7, 24, codes)
         for half in range(2):
-            code = codes[half]
+            solid = lab1[half, x, wide] > 0
             caught = jnp.maximum(sides[half] - reach1[half, x, wide], 0.0)
-            envelope = jnp.where(
-                code > 0, caught, jnp.where(code == 0, grown[half, x, wide], 0.0)
-            )
+            envelope = jnp.where(solid & (codes[half] >= 0), caught, 0.0)
             env1[half, x, wide] = envelope
-            grown1[half, x, wide] = envelope + jnp.where(
-                lab1[half, x, wide] > 0, gspeed[half, x, wide], 0.0
-            )
+            grown1[half, x, wide] = envelope + jnp.where(solid, gspeed[half, x, wide], 0.0)
 
     loop(1, GX - 1, 3, first_growth)
 
@@ -529,15 +535,18 @@
         codes = [lab[2, half, x, own] for half in range(2)]
         sides = pick(grown1, x, 8, GR, codes)
         for half in range(2):
-            code = codes[half]
             caught = jnp.maximum(sides[half] - reach2[half, x, own], 0.0)
-            kept = jnp.where(code == 0, grown1[half, x, own], env1[half, x, own])
-            env_own[x - 2, :, pl.ds(half * NZ, NZ)] = jnp.where(code > 0, caught, kept)
-
-    loop(2, GX - 2, 4, second_growth)
-    env_save = pltpu.make_async_copy(env_own, env_out, save_sem.at[2])
-    env_save.start()
-    for save in (temp_save, grain_save, env_save):
+            env_own[x - 2, :, pl.ds(half * NZ, NZ)] = jnp.where(
+                codes[half] < 0, env1[half, x, own], caught
+            )
+
+    saves = [temp_save, grain_save]
+    for part in range(2):
+        cut = pl.ds(NX // 2 * part, NX // 2)
+        loop(2 + NX // 2 * part, 2 + NX // 2 * (part + 1), 4, second_growth)
+        saves.append(pltpu.make_async_copy(env_own.at[cut], env_out.at[cut], save_sem.at[2 + part]))
+        saves[-1].start()
+    for save in saves:
         save.wait()
 
 
@@ -583,7 +592,7 @@
             pltpu.VMEM((NX, NY, NZ), f32),
             pltpu.VMEM((NX, GR, 2 * NZ), f32),
             pltpu.VMEM((NX, GR, 2 * NZ), i32),
-            dma((3,)),
+            dma((4,)),
             pltpu.VMEM((2, EX, EY, NZ), f32),
             pltpu.VMEM((6, EX, EY, NZ), f32),
             pltpu.VMEM((EX, 8, NZ), f32),
@@ -596,7 +605,6 @@
             pltpu.VMEM((NX, 8, NZ), f32),
             pltpu.VMEM((3,) + growth, i32),
             pltpu.VMEM(growth, i32),
-            pltpu.VMEM(growth, f32),
             pltpu.VMEM(growth, f32),
             pltpu.VMEM(growth, f32),
             pltpu.VMEM(growth, f32),

time: 40.4 us -> 40.3 us (level)
  no operation moved by 1% of the time
where the time goes in v4:
time: 40.3 us; the launch traced here: 40.2 us
  Pallas kernels  39.6 us (98%)
  between operations  0.64 us (2%)
    pallas_call x1, Pallas kernels, body(): pl.pallas_call(kernel, out_shape=results, in_specs=[hbm] * 9, out_specs=(...  37.7 us
    pallas_call x1, Pallas kernels, body(): pl.pallas_call(handing_on, out_shape=results, in_specs=[hbm] * 3, out_spe...  1.88 us

profile of v4, /device:TPU:1, one launch (start us, length us, event | category | flops | bytes accessed | tf_op | source)
XLA Modules:
  0.0 40.2 jit_solution(14786788210382156164)
XLA Ops:
  0.6 37.7 %shard_map.112 = (f32[16,32,128]{2,1,0:T(8,128)}, f32[16,16,256]{2,1,0:T(8,128)}, s32[16,16,256]{2,1,0:T(8,128)}) custom-call(f32[16,32,128]{2,1,0:T(8,128)} %kelvin_hbm.1, f32[16,32,128]{2,1,0:T(8,128)} %conductance_hbm.1, s32[16,32,128]{2,1,0:T(8,128)} %melted_hbm.1, s32[16,16,256]{2,1,0:T(8,128)} %germ_hbm.1, s32[16,16,256]{2,1,0:T(8,128)} %nucleus_hbm.1, ...), custom_call_target="tpu_custom_call" | custom-call | tf_op jit(solution)/shard_map/pallas_call | solution.py:576
  38.3 1.9 %shard_map.113 = (f32[16,32,128]{2,1,0:T(8,128)}, f32[16,16,256]{2,1,0:T(8,128)}, s32[16,16,256]{2,1,0:T(8,128)}) custom-call(f32[16,32,128]{2,1,0:T(8,128)} %get-tuple-element.6.refs_0_, f32[16,16,256]{2,1,0:T(8,128)} %get-tuple-element.7.refs_1_, s32[16,16,256]{2,1,0:T(8,128)} %get-tuple-element.8.refs_2_), custom_call_target="tpu_custom_call" | custom-call | tf_op jit(solution)/shard_map/pallas_call | solution.py:620

commit v5 on v4

--- a/solution.py
+++ b/solution.py
@@ -352,9 +352,9 @@
         strip_out[x] = jnp.where(halo_slot, pltpu.roll(base, (turn + NZ) % NZ, 1), heat)
 
     every = range(EY // 8)
-    loop(0, D, 3, lambda x: pack_halo(x, every, False))
-    loop(D + NX, EX, 3, lambda x: pack_halo(x, every, False))
-    loop(D, D + NX, 4, lambda x: pack_halo(x, (0, EY // 8 - 1), True))
+    loop(0, D, 6, lambda x: pack_halo(x, every, False))
+    loop(D + NX, EX, 6, lambda x: pack_halo(x, every, False))
+    loop(D, D + NX, 8, lambda x: pack_halo(x, (0, EY // 8 - 1), True))
     strip_copy = send(
         strip_out, strip_in, strip_send, strip_recv, at(0, 0, other)
     )
@@ -529,7 +529,7 @@
             env1[half, x, wide] = envelope
             grown1[half, x, wide] = envelope + jnp.where(solid, gspeed[half, x, wide], 0.0)
 
-    loop(1, GX - 1, 3, first_growth)
+    loop(1, GX - 1, 6, first_growth)
 
     def second_growth(x):
         codes = [lab[2, half, x, own] for half in range(2)]
@@ -543,7 +543,7 @@
     saves = [temp_save, grain_save]
     for part in range(2):
         cut = pl.ds(NX // 2 * part, NX // 2)
-        loop(2 + NX // 2 * part, 2 + NX // 2 * (part + 1), 4, second_growth)
+        loop(2 + NX // 2 * part, 2 + NX // 2 * (part + 1), 8, second_growth)
         saves.append(pltpu.make_async_copy(env_own.at[cut], env_out.at[cut], save_sem.at[2 + part]))
         saves[-1].start()
     for save in saves:

time: 40.3 us -> 39.5 us (0.980)
  Pallas kernels: 39.6 us -> 38.7 us
    pallas_call x1, Pallas kernels: 37.7 us -> 36.8 us  [body(): pl.pallas_call(kernel, out_shape=results, in_specs=[hbm] * 9, out_specs=(...]
where the time goes in v5:
time: 39.5 us; the launch traced here: 39.4 us
  Pallas kernels  38.7 us (98%)
  between operations  0.64 us (2%)
    pallas_call x1, Pallas kernels, body(): pl.pallas_call(kernel, out_shape=results, in_specs=[hbm] * 9, out_specs=(...  36.8 us
    pallas_call x1, Pallas kernels, body(): pl.pallas_call(handing_on, out_shape=results, in_specs=[hbm] * 3, out_spe...  1.88 us

profile of v5, /device:TPU:1, one launch (start us, length us, event | category | flops | bytes accessed | tf_op | source)
XLA Modules:
  0.0 39.4 jit_solution(9674910462331794522)
XLA Ops:
  0.6 36.8 %shard_map.112 = (f32[16,32,128]{2,1,0:T(8,128)}, f32[16,16,256]{2,1,0:T(8,128)}, s32[16,16,256]{2,1,0:T(8,128)}) custom-call(f32[16,32,128]{2,1,0:T(8,128)} %kelvin_hbm.1, f32[16,32,128]{2,1,0:T(8,128)} %conductance_hbm.1, s32[16,32,128]{2,1,0:T(8,128)} %melted_hbm.1, s32[16,16,256]{2,1,0:T(8,128)} %germ_hbm.1, s32[16,16,256]{2,1,0:T(8,128)} %nucleus_hbm.1, ...), custom_call_target="tpu_custom_call" | custom-call | tf_op jit(solution)/shard_map/pallas_call | solution.py:576
  37.5 1.9 %shard_map.113 = (f32[16,32,128]{2,1,0:T(8,128)}, f32[16,16,256]{2,1,0:T(8,128)}, s32[16,16,256]{2,1,0:T(8,128)}) custom-call(f32[16,32,128]{2,1,0:T(8,128)} %get-tuple-element.6.refs_0_, f32[16,16,256]{2,1,0:T(8,128)} %get-tuple-element.7.refs_1_, s32[16,16,256]{2,1,0:T(8,128)} %get-tuple-element.8.refs_2_), custom_call_target="tpu_custom_call" | custom-call | tf_op jit(solution)/shard_map/pallas_call | solution.py:620
